TPU v7x, 32 devices: a whole 2x2x4 slice. The times are simulated.
32 devices in a mesh: ep: 16 (over z, x, core), rep: 2 (over y).
Axes of the slice: x: 2, y: 2, z: 4, core: 2. Of those that a mesh axis runs over, the one named last changes fastest.
Arguments:
- tokens_one: bfloat16 [512, 7168], P('ep', 'rep'), may hold values from -6 to 6
- tokens_two: bfloat16 [512, 7168], P('ep', 'rep'), may hold values from -6 to 6
- routes_one: int32 [512, 8], P('ep'), may hold values from 0 to 15, all different within a row; in each aligned block of 32 rows (0 to 31, 32 to 63, ...) at most 32 rows name the same one
- routes_two: int32 [512, 8], P('ep'), may hold values from 0 to 15, all different within a row; in each aligned block of 32 rows (0 to 31, 32 to 63, ...) at most 32 rows name the same one
- gates_one: float32 [512, 8], P('ep'), may hold values from 0.1 to 0.6
- gates_two: float32 [512, 8], P('ep'), may hold values from 0.1 to 0.6
- place_before: int32 [16], replicated, may hold values from 0 to 15, each once
- swap_flags: int32 [8], replicated, may hold values 0 or 1
- gate_weight: bfloat16 [16, 7168, 1024], P('ep', 'rep'), may hold values from -0.0625 to 0.0625
- up_weight: bfloat16 [16, 7168, 1024], P('ep', 'rep'), may hold values from -0.0625 to 0.0625
- down_weight: bfloat16 [16, 1024, 7168], P('ep', None, 'rep'), may hold values from -0.1875 to 0.1875
Outputs:
- mixed_one: bfloat16 [512, 7168], P('ep', 'rep')
- mixed_two: bfloat16 [512, 7168], P('ep', 'rep')
Inputs may be any that keep to these rules, and one draw needn't show every extreme that they name: `routes_one`: in each aligned block of 32 rows (the rows of one index of ep) no expert is named more than 32 times, and in every draw some expert is named exactly 32 times in some block; a row names 8 different experts. `routes_two`: in each aligned block of 32 rows (the rows of one index of ep) no ep index is named more than 32 times, and in every draw some is named exactly 32 times in some block; a row names 8 different ep indices. `place_before`: each ep index appears once.
All inputs are finite; a program needn't handle non-finite values.
Results may differ from a plain program's by a relative error of at most 0.0058.
Values may be sent and summed in bfloat16 or wider, within the bound.
No kernel may reach another device: no remote copies, remote signals or barrier semaphores. Data moves between devices by JAX's collectives and lax.ppermute only.
A program may use at most 128 MiB of HBM per device.

v0:
```python
import functools
import math

import jax
import jax.numpy as jnp
from jax import lax
from jax.experimental import pallas as pl
from jax.experimental.pallas import tpu as pltpu
from jax.sharding import PartitionSpec as P

VMEM_LIMIT = 8 * 1024 * 1024
QUICK = pl.CostEstimate(flops=1, bytes_accessed=1, transcendentals=0)
F32 = jnp.float32
BF16 = jnp.bfloat16
EXTRA = 128
PIECES = 3


def scale_of(extra, step_rows, one, two):
    values = extra.astype(F32)
    names = pltpu.roll(values, EXTRA // 2, 1)
    row = lax.broadcasted_iota(jnp.int32, values.shape, 0)
    lane = lax.broadcasted_iota(jnp.int32, values.shape, 1)
    wanted = jnp.where(row % (2 * step_rows) < step_rows, one, two).astype(F32)
    chosen = jnp.logical_and(names == wanted, lane < EXTRA // 2)
    return jnp.sum(jnp.where(chosen, values, 0.0), axis=1, keepdims=True)


def in_hbm(array):
    return pltpu.with_memory_space_constraint(array, pltpu.HBM)


def in_vmem(array):
    return pltpu.with_memory_space_constraint(array, pltpu.VMEM)


def vmem_limit(*shapes):
    return sum(2 * math.prod(shape) for shape in shapes) + 5 * 1024 * 1024


def load_kernel(count, *refs):
    sems = refs[2 * count]
    copies = [pltpu.make_async_copy(refs[i], refs[count + i], sems.at[i]) for i in range(count)]
    for copy in copies:
        copy.start()
    for copy in copies:
        copy.wait()


def load(arrays, after):
    count = len(arrays)
    any_spec = pl.BlockSpec(memory_space=pl.ANY)
    return pl.pallas_call(
        lambda *refs: load_kernel(count, *refs[:count], *refs[count + len(after) :]),
        out_shape=[pltpu.VMEM(array.shape, array.dtype) for array in arrays],
        in_specs=[any_spec] * (count + len(after)),
        out_specs=[pl.BlockSpec(memory_space=pltpu.VMEM)] * count,
        scratch_shapes=[pltpu.SemaphoreType.DMA((count,))],
        compiler_params=pltpu.CompilerParams(vmem_limit_bytes=VMEM_LIMIT),
        cost_estimate=QUICK,
    )(*[in_hbm(array) for array in arrays], *after)


def sums_kernel(block_count, arrived_count, after_count, part, scalar_ref, *refs):
    block_refs = refs[:block_count]
    gate_ref, up_ref = refs[block_count : block_count + 2]
    arrived_refs = refs[block_count + 2 : block_count + 2 + arrived_count]
    out_ref, rows = refs[block_count + 2 + arrived_count + after_count :]
    depth = rows.shape[1]
    part_width = out_ref.shape[-1]
    tile = 256 if part_width % 256 == 0 else part_width
    start = 0
    for ref in block_refs:
        rows[start : start + ref.shape[0]] = ref[:, :depth]
        start += ref.shape[0]
    for j in range(part_width // tile):
        span = pl.ds(pl.multiple_of(scalar_ref[part] * part_width + j * tile, tile), tile)
        here = slice(j * tile, (j + 1) * tile)
        gate = jnp.dot(rows[...], gate_ref[0, :, span], preferred_element_type=F32)
        up = jnp.dot(rows[...], up_ref[0, :, span], preferred_element_type=F32)
        if arrived_count == 0:
            out_ref[0, :, here] = gate.astype(BF16)
            out_ref[1, :, here] = up.astype(BF16)
        else:
            for ref in arrived_refs:
                gate = gate + ref[0, :, here].astype(F32)
                up = up + ref[1, :, here].astype(F32)
            out_ref[:, here] = (gate / (1.0 + jnp.exp(-gate)) * up).astype(BF16)


def sums(blocks, gate_weight, up_weight, scalars, part, part_width, arrived, after):
    count = sum(block.shape[0] for block in blocks)
    depth = gate_weight.shape[1]
    out_shape = (count, part_width) if arrived else (2, count, part_width)
    any_spec = pl.BlockSpec(memory_space=pl.ANY)
    vmem_spec = pl.BlockSpec(memory_space=pltpu.VMEM)
    return pl.pallas_call(
        functools.partial(sums_kernel, len(blocks), len(arrived), len(after), part),
        out_shape=jax.ShapeDtypeStruct(out_shape, BF16),
        grid_spec=pltpu.PrefetchScalarGridSpec(
            num_scalar_prefetch=1,
            grid=(),
            in_specs=[vmem_spec] * (len(blocks) + 2 + len(arrived)) + [any_spec] * len(after),
            out_specs=vmem_spec,
            scratch_shapes=[pltpu.VMEM((count, depth), BF16)],
        ),
        compiler_params=pltpu.CompilerParams(
            vmem_limit_bytes=vmem_limit(
                (count, depth), *[block.shape for block in blocks], *[pair.shape for pair in arrived], out_shape
            )
        ),
        cost_estimate=QUICK,
    )(scalars, *blocks, in_vmem(gate_weight), in_vmem(up_weight), *arrived, *after)


def down_kernel(parts, block_count, after_count, step_rows, scalar_ref, *refs):
    hidden_refs = refs[:parts]
    down_ref = refs[parts]
    block_refs = refs[parts + 1 : parts + 1 + block_count]
    near_ref, far_ref, sent_near_ref, sent_far_ref, hidden = refs[parts + 1 + block_count + after_count :]
    part_width = hidden_refs[0].shape[1]
    width = down_ref.shape[2]
    for p, ref in enumerate(hidden_refs):
        start = pl.multiple_of(scalar_ref[2 + p] * part_width, part_width)
        hidden[:, pl.ds(start, part_width)] = ref[...]
    scale = jnp.concatenate(
        [scale_of(ref[:, width:], step_rows, scalar_ref[0], scalar_ref[1]) for ref in block_refs], axis=0
    )
    quarter = scale.shape[0] // 4
    tile = 512 if width % 512 == 0 else 256
    for j in range(width // tile):
        here = slice(j * tile, (j + 1) * tile)
        total = jnp.dot(hidden[...], down_ref[0, :, here], preferred_element_type=F32) * scale
        for i, ref in enumerate((near_ref, far_ref, sent_near_ref, sent_far_ref)):
            ref[:, here] = total[i * quarter : (i + 1) * quarter].astype(ref.dtype)


def down_rows(hidden_parts, down_weight, blocks, step_rows, scalars, after):
    parts = len(hidden_parts)
    count, part_width = hidden_parts[0].shape
    width = down_weight.shape[2]
    any_spec = pl.BlockSpec(memory_space=pl.ANY)
    vmem_spec = pl.BlockSpec(memory_space=pltpu.VMEM)
    return pl.pallas_call(
        functools.partial(down_kernel, parts, len(blocks), len(after), step_rows),
        out_shape=[jax.ShapeDtypeStruct((count // 4, width), dtype) for dtype in (F32, F32, BF16, BF16)],
        grid_spec=pltpu.PrefetchScalarGridSpec(
            num_scalar_prefetch=1,
            grid=(),
            in_specs=[vmem_spec] * (parts + 1 + len(blocks)) + [any_spec] * len(after),
            out_specs=[vmem_spec] * 4,
            scratch_shapes=[pltpu.VMEM((count, parts * part_width), BF16)],
        ),
        compiler_params=pltpu.CompilerParams(
            vmem_limit_bytes=vmem_limit(
                (2 * count, parts * part_width), *[block.shape for block in blocks], (3 * count // 2, width)
            )
        ),
        cost_estimate=QUICK,
    )(scalars, *hidden_parts, in_vmem(down_weight), *blocks, *after)


def base_kernel(one_ref, two_ref, route_one_ref, route_two_ref, gate_one_ref, gate_two_ref, out_ref):
    step_rows, width = one_ref.shape
    top = route_one_ref.shape[0]
    out_ref[:step_rows, :width] = one_ref[...]
    out_ref[step_rows:, :width] = two_ref[...]
    column = lax.broadcasted_iota(jnp.int32, (top, EXTRA), 1)
    choice = lax.broadcasted_iota(jnp.int32, (top, EXTRA), 0)

    def placed(value, start):
        where = (column == choice + start).astype(BF16)
        return lax.dot_general(
            value.astype(BF16), where, (((0,), (0,)), ((), ())), preferred_element_type=F32
        )

    for place, route_ref, gate_ref in ((0, route_one_ref, gate_one_ref), (1, route_two_ref, gate_two_ref)):
        rest = gate_ref[...]
        names = route_ref[...].astype(F32)
        total = None
        for piece in range(PIECES):
            part = rest.astype(BF16).astype(F32)
            rest = rest - part
            term = placed(part, piece * top) + placed(names, EXTRA // 2 + piece * top)
            total = term if total is None else total + term
        out_ref[place * step_rows : (place + 1) * step_rows, width:] = total.astype(BF16)


def base_rows(tokens_one, tokens_two, routes_one, routes_two, gates_one, gates_two):
    step_rows, width = tokens_one.shape
    return pl.pallas_call(
        base_kernel,
        out_shape=jax.ShapeDtypeStruct((2 * step_rows, width + EXTRA), BF16),
        in_specs=[pl.BlockSpec(memory_space=pltpu.VMEM)] * 6,
        out_specs=pl.BlockSpec(memory_space=pltpu.VMEM),
        compiler_params=pltpu.CompilerParams(vmem_limit_bytes=VMEM_LIMIT),
    )(*[in_hbm(array) for array in (tokens_one, tokens_two, routes_one.T, routes_two.T, gates_one.T, gates_two.T)])


def shifted(value, axis, size, step):
    return lax.ppermute(value, axis, [(i, (i + step) % size) for i in range(size)])


def flipped(value, size, bits):
    return lax.ppermute(value, "ep", [(i, i ^ bits) for i in range(size)])


def shards(
    tokens_one,
    tokens_two,
    routes_one,
    routes_two,
    gates_one,
    gates_two,
    place_before,
    swap_flags,
    gate_weight,
    up_weight,
    down_weight,
):
    ep = lax.axis_size("ep")
    rep = lax.axis_size("rep")
    me = lax.axis_index("ep")
    y = lax.axis_index("rep")
    half = ep // 2
    z_count = ep // 4
    row_count, width = tokens_one.shape
    part_width = gate_weight.shape[2] // rep
    indices = jnp.arange(ep, dtype=jnp.int32)

    part_ids = [y] + [(y - step) % rep for step in range(1, rep)]
    turn_ids = [(y + step) % rep for step in range(1, rep)]
    expert = jnp.sum(jnp.where(place_before == me, indices, 0))
    flag = jnp.sum(jnp.where(indices[:half] == me % half, swap_flags, 0))
    after = jnp.where(flag == 1, jnp.where(me < half, me + half, me - half), me)
    scalars = jnp.stack([expert, after] + part_ids + turn_ids).astype(jnp.int32)

    both = base_rows(tokens_one, tokens_two, routes_one, routes_two, gates_one, gates_two)

    groups = 4
    per_group = z_count // groups
    members = [[group * per_group + i for i in range(per_group)] for group in (0, 2, 3, 1)]
    early = {0: both}
    for group in (members[0], members[1], members[3], members[2]):
        for r in group:
            early[r] = early.get(r) if r == 0 else flipped(both, ep, 4 * r)
    along_z = [[early[r] for r in group] for group in members]
    gate_weight, up_weight = load([gate_weight, up_weight], [both, scalars])
    (down_weight,) = load([down_weight], [gate_weight])
    state = [dict() for _ in range(groups)]
    last = [down_weight]

    def follow(*values):
        held = lax.optimization_barrier(tuple(values) + tuple(last))
        return held[: len(values)]

    def ask_x(g):
        near = along_z[g] if g == 0 else follow(*along_z[g])
        state[g]["near"] = list(near)
        state[g]["across"] = [flipped(value, ep, 2) for value in near]

    def ask_core(g):
        across = list(follow(*state[g]["across"]))
        here = state[g]["near"] + across
        state[g]["blocks"] = here + [flipped(value, ep, 1) for value in here]

    def hold_z(g):
        last.extend(along_z[g])

    def hold_x(g):
        last.extend(state[g]["across"])

    def hold_core(g):
        last.append(state[g]["core_far"])

    def send_sums(g):
        state[g]["arrived"] = []
        for step in range(1, rep):
            partial = sums(
                state[g]["blocks"], gate_weight, up_weight, scalars, 1 + rep + step, part_width, [], last
            )
            last[:] = [partial]
            state[g]["arrived"].append(shifted(partial, "rep", rep, step))

    def send_hidden(g):
        hidden = sums(
            state[g]["blocks"], gate_weight, up_weight, scalars, 2, part_width, state[g]["arrived"], last
        )
        last[:] = [hidden]
        state[g]["hidden"] = [hidden] + [shifted(hidden, "rep", rep, step) for step in range(1, rep)]

    def send_core(g):
        near, far, sent_near, sent_far = down_rows(
            state[g]["hidden"], down_weight, state[g]["blocks"], row_count, scalars, last
        )
        last[:] = [sent_far]
        state[g]["own"] = near, far
        state[g]["core_far"] = flipped(sent_far, ep, 1)
        state[g]["core_near"] = flipped(sent_near, ep, 1)

    def send_x(g):
        (core,) = follow(state[g]["core_far"])
        far = (state[g]["own"][1] + core.astype(F32)).astype(BF16)
        last.append(far)
        state[g]["x"] = flipped(far, ep, 2)

    def send_z(g):
        core, across = follow(state[g]["core_near"], state[g]["x"])
        near = state[g]["own"][0] + core.astype(F32) + across.astype(F32)
        near = near.reshape(per_group, 2 * row_count, width)
        state[g]["z"] = []
        for place, r in enumerate(members[g]):
            if r == 0:
                last.append(near[place])
                state[g]["z"].append(near[place])
            else:
                block = near[place].astype(BF16)
                last.append(block)
                state[g]["z"].append(flipped(block, ep, 4 * r))

    totals = []

    def finish(g):
        total = totals[-1] if totals else None
        for block in state[g]["z"]:
            total = block.astype(F32) if total is None else total + block.astype(F32)
        totals.append(total)
        last.append(total)

    def run(*turns):
        for stage, g in turns:
            stage(g)

    run((ask_x, 0), (ask_core, 0), (hold_z, 1), (send_sums, 0), (ask_x, 1), (hold_x, 1), (send_hidden, 0), (ask_core, 1))
    run((hold_z, 2), (send_sums, 1), (ask_x, 2), (send_core, 0), (hold_x, 2), (send_hidden, 1), (hold_core, 0), (hold_z, 3))
    run((ask_core, 2), (ask_x, 3), (send_sums, 2), (hold_x, 3), (send_core, 1), (send_hidden, 2), (send_x, 1))
    run((ask_core, 3), (send_sums, 3), (send_core, 2), (send_z, 1), (send_x, 0), (send_hidden, 3), (send_x, 2))
    run((send_core, 3), (send_z, 0), (finish, 0), (finish, 1), (send_x, 3), (send_z, 2), (send_z, 3), (finish, 2), (finish, 3))
    total = totals[-1]
    return total[:row_count].astype(BF16), total[row_count:].astype(BF16)


def solution(mesh):
    return jax.shard_map(
        shards,
        mesh=mesh,
        in_specs=(
            P("ep", "rep"),
            P("ep", "rep"),
            P("ep", None),
            P("ep", None),
            P("ep", None),
            P("ep", None),
            P(),
            P(),
            P("ep", "rep", None),
            P("ep", "rep", None),
            P("ep", None, "rep"),
        ),
        out_specs=(P("ep", "rep"), P("ep", "rep")),
        check_vma=False,
    )
```

profile of v0, /device:TPU:0, one launch (start us, length us, event | category | flops | bytes accessed | tf_op | source)
XLA Modules:
  0.0 163.2 jit_solution(15114348863868868850)
XLA Ops:
  1.9 3.0 %collective-permute-start = (bf16[64,3712]{1,0:T(8,128)(2,1)S(1)}, bf16[64,3712]{1,0:T(8,128)(2,1)S(1)}, u32[]{:S(2)}, u32[]{:S(2)}) collective-permute-start(bf16[64,3712]{1,0:T(8,128)(2,1)S(1)} %shard_map.122.refs_2_.refs_0_.refs_3_), channel_id=1, source_target_pairs={{0,4},{2,6},{4,0},{6,2},{8,12},{10,14},{12,8},{14,10},{16,20},{18,... | collective-permute-start | bytes 1425416 | tf_op jit(solution)/shard_map/ppermute | solution.py:205
  4.9 2.6 %collective-permute-start.3 = (bf16[64,3712]{1,0:T(8,128)(2,1)S(1)}, bf16[64,3712]{1,0:T(8,128)(2,1)S(1)}, u32[]{:S(2)}, u32[]{:S(2)}) collective-permute-start(bf16[64,3712]{1,0:T(8,128)(2,1)S(1)} %shard_map.122.refs_2_.refs_0_.refs_3_), channel_id=1, source_target_pairs={{0,16},{2,18},{4,20},{6,22},{8,24},{10,26},{12,28},{14,30},{16,0},... | collective-permute-start | bytes 1425416 | tf_op jit(solution)/shard_map/ppermute | solution.py:205
  11.5 5.2 %shard_map.123 = (bf16[1,3584,1024]{2,1,0:T(8,128)(2,1)S(1)}, bf16[1,3584,1024]{2,1,0:T(8,128)(2,1)S(1)}) custom-call(bf16[1,3584,1024]{2,1,0:T(8,128)(2,1)} %refs_0_.2, bf16[1,3584,1024]{2,1,0:T(8,128)(2,1)} %refs_1_.1, bf16[64,3712]{1,0:T(8,128)(2,1)S(1)} %shard_map.122.refs_2_.refs_0_.refs_3_, s32[5]{0:T(128)S(1)} %stack.23.refs_3_.scalar_ref), custom_call_target="tpu_custom_call" | custom-call | flops 1 | bytes 1 | tf_op jit(solution)/shard_map/pallas_call | solution.py:53
  16.7 3.1 %shard_map.124.refs_6_.refs_2_ = bf16[1,1024,3584]{2,1,0:T(8,128)(2,1)S(1)} custom-call(bf16[1,1024,3584]{2,1,0:T(8,128)(2,1)} %refs_0_.3, bf16[1,3584,1024]{2,1,0:T(8,128)(2,1)S(1)} %get-tuple-element.39.refs_1_.refs_4_), custom_call_target="tpu_custom_call" | custom-call | flops 1 | bytes 1 | tf_op jit(solution)/shard_map/pallas_call | solution.py:53
  20.4 7.9 %collective-permute-done.3.refs_7_.refs_0_.refs_3_ = bf16[64,3712]{1,0:T(8,128)(2,1)S(1)} collective-permute-done((bf16[64,3712]{1,0:T(8,128)(2,1)S(1)}, bf16[64,3712]{1,0:T(8,128)(2,1)S(1)}, u32[]{:S(2)}, u32[]{:S(2)}) %collective-permute-start.3) | collective-permute-done | bytes 475168 | tf_op jit(solution)/shard_map/ppermute | solution.py:205
  28.4 2.7 %shard_map.125.refs_7_ = bf16[2,256,512]{2,1,0:T(8,128)(2,1)S(1)} custom-call(s32[5]{0:T(128)S(1)} %stack.23.refs_3_.scalar_ref, bf16[64,3712]{1,0:T(8,128)(2,1)S(1)} %shard_map.122.refs_2_.refs_0_.refs_3_, bf16[64,3712]{1,0:T(8,128)(2,1)S(1)} %collective-permute-done.refs_1_.refs_4_, bf16[64,3712]{1,0:T(8,128)(2,1)S(1)} %collective-permute-done.1.refs_2_.refs_5_, ...), custom_call_target="tpu_custom_call" | custom-call | flops 1 | bytes 1 | tf_op jit(solution)/shard_map/pallas_call | solution.py:97
  33.2 3.5 %collective-permute-start.9 = (bf16[64,3712]{1,0:T(8,128)(2,1)S(1)}, bf16[64,3712]{1,0:T(8,128)(2,1)S(1)}, u32[]{:S(2)}, u32[]{:S(2)}) collective-permute-start(bf16[64,3712]{1,0:T(8,128)(2,1)S(1)} %shard_map.122.refs_2_.refs_0_.refs_3_), channel_id=1, source_target_pairs={{0,24},{2,26},{4,28},{6,30},{8,16},{10,18},{12,20},{14,22},{16,8},... | collective-permute-start | bytes 1425416 | tf_op jit(solution)/shard_map/ppermute | solution.py:205
  36.7 7.4 %collective-permute-done.5.refs_8_.refs_1_.refs_4_ = bf16[64,3712]{1,0:T(8,128)(2,1)S(1)} collective-permute-done((bf16[64,3712]{1,0:T(8,128)(2,1)S(1)}, bf16[64,3712]{1,0:T(8,128)(2,1)S(1)}, u32[]{:S(2)}, u32[]{:S(2)}) %collective-permute-start.5) | collective-permute-done | bytes 475168 | tf_op jit(solution)/shard_map/ppermute | solution.py:205
  44.1 2.8 %shard_map.126.refs_6_.refs_0_ = bf16[256,512]{1,0:T(8,128)(2,1)S(1)} custom-call(s32[5]{0:T(128)S(1)} %stack.23.refs_3_.scalar_ref, bf16[64,3712]{1,0:T(8,128)(2,1)S(1)} %shard_map.122.refs_2_.refs_0_.refs_3_, bf16[64,3712]{1,0:T(8,128)(2,1)S(1)} %collective-permute-done.refs_1_.refs_4_, bf16[64,3712]{1,0:T(8,128)(2,1)S(1)} %collective-permute-done.1.refs_2_.refs_5_, ...), custom_call_target="tpu_custom_call" | custom-call | flops 1 | bytes 1 | tf_op jit(solution)/shard_map/pallas_call | solution.py:97
  48.8 2.7 %shard_map.127.refs_7_ = bf16[2,256,512]{2,1,0:T(8,128)(2,1)S(1)} custom-call(s32[5]{0:T(128)S(1)} %stack.23.refs_3_.scalar_ref, bf16[64,3712]{1,0:T(8,128)(2,1)S(1)} %collective-permute-done.3.refs_7_.refs_0_.refs_3_, bf16[64,3712]{1,0:T(8,128)(2,1)S(1)} %collective-permute-done.5.refs_8_.refs_1_.refs_4_, ...), custom_call_target="tpu_custom_call" | custom-call | flops 1 | bytes 1 | tf_op jit(solution)/shard_map/pallas_call | solution.py:97
  53.4 7.6 %collective-permute-start.14 = (bf16[64,3712]{1,0:T(8,128)(2,1)S(1)}, bf16[64,3712]{1,0:T(8,128)(2,1)S(1)}, u32[]{:S(2)}, u32[]{:S(2)}) collective-permute-start(bf16[64,3712]{1,0:T(8,128)(2,1)S(1)} %shard_map.122.refs_2_.refs_0_.refs_3_), channel_id=1, source_target_pairs={{0,8},{2,10},{4,12},{6,14},{8,0},{10,2},{12,4},{14,6},{16,24},{18,... | collective-permute-start | bytes 1425416 | tf_op jit(solution)/shard_map/ppermute | solution.py:205
  61.0 2.7 %shard_map.128 = (f32[64,3584]{1,0:T(8,128)S(1)}, f32[64,3584]{1,0:T(8,128)S(1)}, bf16[64,3584]{1,0:T(8,128)(2,1)S(1)}, bf16[64,3584]{1,0:T(8,128)(2,1)S(1)}) custom-call(s32[5]{0:T(128)S(1)} %stack.23.refs_3_.scalar_ref, bf16[256,512]{1,0:T(8,128)(2,1)S(1)} %shard_map.126.refs_6_.refs_0_, bf16[256,512]{1,0:T(8,128)(2,1)S(1)} %collective-permute-done.6.refs_1_, ...), custom_call_target="tpu_custom_call" | custom-call | flops 1 | bytes 1 | tf_op jit(solution)/shard_map/pallas_call | solution.py:144
  66.9 2.8 %shard_map.129.refs_6_.refs_0_ = bf16[256,512]{1,0:T(8,128)(2,1)S(1)} custom-call(s32[5]{0:T(128)S(1)} %stack.23.refs_3_.scalar_ref, bf16[64,3712]{1,0:T(8,128)(2,1)S(1)} %collective-permute-done.3.refs_7_.refs_0_.refs_3_, bf16[64,3712]{1,0:T(8,128)(2,1)S(1)} %collective-permute-done.5.refs_8_.refs_1_.refs_4_, ...), custom_call_target="tpu_custom_call" | custom-call | flops 1 | bytes 1 | tf_op jit(solution)/shard_map/pallas_call | solution.py:97
  72.1 2.7 %shard_map.130.refs_7_ = bf16[2,256,512]{2,1,0:T(8,128)(2,1)S(1)} custom-call(s32[5]{0:T(128)S(1)} %stack.23.refs_3_.scalar_ref, bf16[64,3712]{1,0:T(8,128)(2,1)S(1)} %collective-permute-done.9.refs_7_.refs_0_.refs_3_, bf16[64,3712]{1,0:T(8,128)(2,1)S(1)} %collective-permute-done.12.refs_8_.refs_1_.refs_4_, ...), custom_call_target="tpu_custom_call" | custom-call | flops 1 | bytes 1 | tf_op jit(solution)/shard_map/pallas_call | solution.py:97
  76.2 3.5 %collective-permute-done.18.refs_1_ = bf16[256,512]{1,0:T(8,128)(2,1)S(1)} collective-permute-done((bf16[256,512]{1,0:T(8,128)(2,1)S(1)}, bf16[256,512]{1,0:T(8,128)(2,1)S(1)}, u32[]{:S(2)}, u32[]{:S(2)}) %collective-permute-start.18) | collective-permute-done | bytes 262176 | tf_op jit(solution)/shard_map/ppermute | solution.py:201
  79.7 3.6 %collective-permute-done.19.refs_8_.refs_1_.refs_4_ = bf16[64,3712]{1,0:T(8,128)(2,1)S(1)} collective-permute-done((bf16[64,3712]{1,0:T(8,128)(2,1)S(1)}, bf16[64,3712]{1,0:T(8,128)(2,1)S(1)}, u32[]{:S(2)}, u32[]{:S(2)}) %collective-permute-start.19) | collective-permute-done | bytes 475168 | tf_op jit(solution)/shard_map/ppermute | solution.py:205
  83.3 2.9 %shard_map.131 = (f32[64,3584]{1,0:T(8,128)S(1)}, f32[64,3584]{1,0:T(8,128)S(1)}, bf16[64,3584]{1,0:T(8,128)(2,1)S(1)}, bf16[64,3584]{1,0:T(8,128)(2,1)S(1)}) custom-call(s32[5]{0:T(128)S(1)} %stack.23.refs_3_.scalar_ref, bf16[256,512]{1,0:T(8,128)(2,1)S(1)} %shard_map.129.refs_6_.refs_0_, bf16[256,512]{1,0:T(8,128)(2,1)S(1)} %collective-permute-done.18.refs_1_, ...), custom_call_target="tpu_custom_call" | custom-call | flops 1 | bytes 1 | tf_op jit(solution)/shard_map/pallas_call | solution.py:144
  86.9 3.4 %collective-permute-done.17.refs_6_ = bf16[2,256,512]{2,1,0:T(8,128)(2,1)S(1)} collective-permute-done((bf16[2,256,512]{2,1,0:T(8,128)(2,1)S(1)}, bf16[2,256,512]{2,1,0:T(8,128)(2,1)S(1)}, u32[]{:S(2)}, u32[]{:S(2)}) %collective-permute-start.17) | collective-permute-done | bytes 524320 | tf_op jit(solution)/shard_map/ppermute | solution.py:201
  90.3 2.8 %shard_map.132.refs_6_.refs_0_ = bf16[256,512]{1,0:T(8,128)(2,1)S(1)} custom-call(s32[5]{0:T(128)S(1)} %stack.23.refs_3_.scalar_ref, bf16[64,3712]{1,0:T(8,128)(2,1)S(1)} %collective-permute-done.9.refs_7_.refs_0_.refs_3_, bf16[64,3712]{1,0:T(8,128)(2,1)S(1)} %collective-permute-done.12.refs_8_.refs_1_.refs_4_, ...), custom_call_target="tpu_custom_call" | custom-call | flops 1 | bytes 1 | tf_op jit(solution)/shard_map/pallas_call | solution.py:97
  96.7 2.7 %shard_map.133.refs_7_ = bf16[2,256,512]{2,1,0:T(8,128)(2,1)S(1)} custom-call(s32[5]{0:T(128)S(1)} %stack.23.refs_3_.scalar_ref, bf16[64,3712]{1,0:T(8,128)(2,1)S(1)} %collective-permute-done.14.refs_8_.refs_0_.refs_3_, bf16[64,3712]{1,0:T(8,128)(2,1)S(1)} %collective-permute-done.19.refs_8_.refs_1_.refs_4_, ...), custom_call_target="tpu_custom_call" | custom-call | flops 1 | bytes 1 | tf_op jit(solution)/shard_map/pallas_call | solution.py:97
  100.0 3.7 %collective-permute-done.20.refs_1_ = bf16[256,512]{1,0:T(8,128)(2,1)S(1)} collective-permute-done((bf16[256,512]{1,0:T(8,128)(2,1)S(1)}, bf16[256,512]{1,0:T(8,128)(2,1)S(1)}, u32[]{:S(2)}, u32[]{:S(2)}) %collective-permute-start.20) | collective-permute-done | bytes 262176 | tf_op jit(solution)/shard_map/ppermute | solution.py:201
  103.8 2.7 %shard_map.134 = (f32[64,3584]{1,0:T(8,128)S(1)}, f32[64,3584]{1,0:T(8,128)S(1)}, bf16[64,3584]{1,0:T(8,128)(2,1)S(1)}, bf16[64,3584]{1,0:T(8,128)(2,1)S(1)}) custom-call(s32[5]{0:T(128)S(1)} %stack.23.refs_3_.scalar_ref, bf16[256,512]{1,0:T(8,128)(2,1)S(1)} %shard_map.132.refs_6_.refs_0_, bf16[256,512]{1,0:T(8,128)(2,1)S(1)} %collective-permute-done.20.refs_1_, ...), custom_call_target="tpu_custom_call" | custom-call | flops 1 | bytes 1 | tf_op jit(solution)/shard_map/pallas_call | solution.py:144
  106.8 5.0 %collective-permute-start.30 = (bf16[64,3584]{1,0:T(8,128)(2,1)S(1)}, bf16[64,3584]{1,0:T(8,128)(2,1)S(1)}, u32[]{:S(2)}, u32[]{:S(2)}) collective-permute-start(bf16[64,3584]{1,0:T(8,128)(2,1)S(1)} %add_convert_fusion.6.refs_8_), channel_id=1, source_target_pairs={{0,16},{2,18},{4,20},{6,22},{8,24},{10,26},{12,28},{14,30},{16,0},... | collective-permute-start | bytes 1376264 | tf_op jit(solution)/shard_map/ppermute | solution.py:205
  114.5 2.8 %shard_map.135.refs_0_.refs_7_ = bf16[256,512]{1,0:T(8,128)(2,1)S(1)} custom-call(s32[5]{0:T(128)S(1)} %stack.23.refs_3_.scalar_ref, bf16[64,3712]{1,0:T(8,128)(2,1)S(1)} %collective-permute-done.14.refs_8_.refs_0_.refs_3_, bf16[64,3712]{1,0:T(8,128)(2,1)S(1)} %collective-permute-done.19.refs_8_.refs_1_.refs_4_, ...), custom_call_target="tpu_custom_call" | custom-call | flops 1 | bytes 1 | tf_op jit(solution)/shard_map/pallas_call | solution.py:97
  118.9 7.1 %collective-permute-done.28.refs_1_ = bf16[256,512]{1,0:T(8,128)(2,1)S(1)} collective-permute-done((bf16[256,512]{1,0:T(8,128)(2,1)S(1)}, bf16[256,512]{1,0:T(8,128)(2,1)S(1)}, u32[]{:S(2)}, u32[]{:S(2)}) %collective-permute-start.28) | collective-permute-done | bytes 262176 | tf_op jit(solution)/shard_map/ppermute | solution.py:201
  126.6 2.7 %shard_map.136 = (f32[64,3584]{1,0:T(8,128)S(1)}, f32[64,3584]{1,0:T(8,128)S(1)}, bf16[64,3584]{1,0:T(8,128)(2,1)S(1)}, bf16[64,3584]{1,0:T(8,128)(2,1)S(1)}) custom-call(s32[5]{0:T(128)S(1)} %stack.23.refs_3_.scalar_ref, bf16[256,512]{1,0:T(8,128)(2,1)S(1)} %shard_map.135.refs_0_.refs_7_, bf16[256,512]{1,0:T(8,128)(2,1)S(1)} %collective-permute-done.28.refs_1_, ...), custom_call_target="tpu_custom_call" | custom-call | flops 1 | bytes 1 | tf_op jit(solution)/shard_map/pallas_call | solution.py:144
  129.9 2.9 %collective-permute-done.30 = bf16[64,3584]{1,0:T(8,128)(2,1)S(1)} collective-permute-done((bf16[64,3584]{1,0:T(8,128)(2,1)S(1)}, bf16[64,3584]{1,0:T(8,128)(2,1)S(1)}, u32[]{:S(2)}, u32[]{:S(2)}) %collective-permute-start.30) | collective-permute-done | bytes 458784 | tf_op jit(solution)/shard_map/ppermute | solution.py:205
  134.6 4.9 %collective-permute-done.32 = bf16[64,3584]{1,0:T(8,128)(2,1)S(1)} collective-permute-done((bf16[64,3584]{1,0:T(8,128)(2,1)S(1)}, bf16[64,3584]{1,0:T(8,128)(2,1)S(1)}, u32[]{:S(2)}, u32[]{:S(2)}) %collective-permute-start.32) | collective-permute-done | bytes 458784 | tf_op jit(solution)/shard_map/ppermute | solution.py:205
  139.7 4.4 %collective-permute-start.34 = (bf16[64,3584]{1,0:T(8,128)(2,1)S(1)}, bf16[64,3584]{1,0:T(8,128)(2,1)S(1)}, u32[]{:S(2)}, u32[]{:S(2)}) collective-permute-start(bf16[64,3584]{1,0:T(8,128)(2,1)S(1)} %add_convert_fusion.2), channel_id=1, source_target_pairs={{0,24},{2,26},{4,28},{6,30},{8,16},{10,18},{12,20},{14,22},{16,8},... | collective-permute-start | bytes 1376264 | tf_op jit(solution)/shard_map/ppermute | solution.py:205
  144.1 4.0 %collective-permute-done.36 = bf16[64,3584]{1,0:T(8,128)(2,1)S(1)} collective-permute-done((bf16[64,3584]{1,0:T(8,128)(2,1)S(1)}, bf16[64,3584]{1,0:T(8,128)(2,1)S(1)}, u32[]{:S(2)}, u32[]{:S(2)}) %collective-permute-start.36) | collective-permute-done | bytes 458784 | tf_op jit(solution)/shard_map/ppermute | solution.py:205
  148.2 4.3 %collective-permute-start.37 = (bf16[64,3584]{1,0:T(8,128)(2,1)S(1)}, bf16[64,3584]{1,0:T(8,128)(2,1)S(1)}, u32[]{:S(2)}, u32[]{:S(2)}) collective-permute-start(bf16[64,3584]{1,0:T(8,128)(2,1)S(1)} %add_convert_fusion.1), channel_id=1, source_target_pairs={{0,8},{2,10},{4,12},{6,14},{8,0},{10,2},{12,4},{14,6},{16,24},{18,... | collective-permute-start | bytes 1376264 | tf_op jit(solution)/shard_map/ppermute | solution.py:205
  152.5 9.7 %collective-permute-done.37 = bf16[64,3584]{1,0:T(8,128)(2,1)S(1)} collective-permute-done((bf16[64,3584]{1,0:T(8,128)(2,1)S(1)}, bf16[64,3584]{1,0:T(8,128)(2,1)S(1)}, u32[]{:S(2)}, u32[]{:S(2)}) %collective-permute-start.37) | collective-permute-done | bytes 458784 | tf_op jit(solution)/shard_map/ppermute | solution.py:205
  (73 shorter events, 31.7 us)
Async XLA Ops:
  1.9 17.9 %collective-permute-start = (bf16[64,3712]{1,0:T(8,128)(2,1)S(1)}, bf16[64,3712]{1,0:T(8,128)(2,1)S(1)}, u32[]{:S(2)}, u32[]{:S(2)}) collective-permute-start(bf16[64,3712]{1,0:T(8,128)(2,1)S(1)} %shard_map.122.refs_2_.refs_0_.refs_3_), channel_id=1, source_target_pairs={{0,4},{2,6},{4,0},{6,2},{8,12},{10,14},{12,8},{14,10},{16,20},{18,... | collective-permute-start | bytes 1425416 | tf_op jit(solution)/shard_map/ppermute | solution.py:205
  4.9 23.4 %collective-permute-start.3 = (bf16[64,3712]{1,0:T(8,128)(2,1)S(1)}, bf16[64,3712]{1,0:T(8,128)(2,1)S(1)}, u32[]{:S(2)}, u32[]{:S(2)}) collective-permute-start(bf16[64,3712]{1,0:T(8,128)(2,1)S(1)} %shard_map.122.refs_2_.refs_0_.refs_3_), channel_id=1, source_target_pairs={{0,16},{2,18},{4,20},{6,22},{8,24},{10,26},{12,28},{14,30},{16,0},... | collective-permute-start | bytes 1425416 | tf_op jit(solution)/shard_map/ppermute | solution.py:205
  7.5 20.8 %collective-permute-start.1 = (bf16[64,3712]{1,0:T(8,128)(2,1)S(1)}, bf16[64,3712]{1,0:T(8,128)(2,1)S(1)}, u32[]{:S(2)}, u32[]{:S(2)}) collective-permute-start(bf16[64,3712]{1,0:T(8,128)(2,1)S(1)} %shard_map.122.refs_2_.refs_0_.refs_3_), channel_id=1, source_target_pairs={{0,2},{2,0},{4,6},{6,4},{8,10},{10,8},{12,14},{14,12},{16,18},{18,... | collective-permute-start | bytes 1425416 | tf_op jit(solution)/shard_map/ppermute | solution.py:205
  19.9 8.5 %collective-permute-start.2 = (bf16[64,3712]{1,0:T(8,128)(2,1)S(1)}, bf16[64,3712]{1,0:T(8,128)(2,1)S(1)}, u32[]{:S(2)}, u32[]{:S(2)}) collective-permute-start(bf16[64,3712]{1,0:T(8,128)(2,1)S(1)} %collective-permute-done.refs_1_.refs_4_), channel_id=1, source_target_pairs={{0,2},{2,0},{4,6},{6,4},{8,10},{10,8},{12,14},{14,12},{16,18},{18,... | collective-permute-start | bytes 1425416 | tf_op jit(solution)/shard_map/ppermute | solution.py:205
  31.0 13.1 %collective-permute-start.4 = (bf16[2,256,512]{2,1,0:T(8,128)(2,1)S(1)}, bf16[2,256,512]{2,1,0:T(8,128)(2,1)S(1)}, u32[]{:S(2)}, u32[]{:S(2)}) collective-permute-start(bf16[2,256,512]{2,1,0:T(8,128)(2,1)S(1)} %shard_map.125.refs_7_), channel_id=1, source_target_pairs={{0,1},{1,0},{2,3},{3,2},{4,5},{5,4},{6,7},{7,6},{8,9},{9,8},{10,11... | collective-permute-start | bytes 1572872 | tf_op jit(solution)/shard_map/ppermute | solution.py:201
  32.7 11.4 %collective-permute-start.5 = (bf16[64,3712]{1,0:T(8,128)(2,1)S(1)}, bf16[64,3712]{1,0:T(8,128)(2,1)S(1)}, u32[]{:S(2)}, u32[]{:S(2)}) collective-permute-start(bf16[64,3712]{1,0:T(8,128)(2,1)S(1)} %collective-permute-done.3.refs_7_.refs_0_.refs_3_), channel_id=1, source_target_pairs={{0,4},{2,6},{4,0},{6,2},{8,12},{10,14},{12,8},{14,10},{16,20},{18,... | collective-permute-start | bytes 1425416 | tf_op jit(solution)/shard_map/ppermute | solution.py:205
  33.2 15.1 %collective-permute-start.9 = (bf16[64,3712]{1,0:T(8,128)(2,1)S(1)}, bf16[64,3712]{1,0:T(8,128)(2,1)S(1)}, u32[]{:S(2)}, u32[]{:S(2)}) collective-permute-start(bf16[64,3712]{1,0:T(8,128)(2,1)S(1)} %shard_map.122.refs_2_.refs_0_.refs_3_), channel_id=1, source_target_pairs={{0,24},{2,26},{4,28},{6,30},{8,16},{10,18},{12,20},{14,22},{16,8},... | collective-permute-start | bytes 1425416 | tf_op jit(solution)/shard_map/ppermute | solution.py:205
  36.7 11.6 %collective-permute-start.7 = (bf16[64,3712]{1,0:T(8,128)(2,1)S(1)}, bf16[64,3712]{1,0:T(8,128)(2,1)S(1)}, u32[]{:S(2)}, u32[]{:S(2)}) collective-permute-start(bf16[64,3712]{1,0:T(8,128)(2,1)S(1)} %collective-permute-done.3.refs_7_.refs_0_.refs_3_), channel_id=1, source_target_pairs={{0,2},{2,0},{4,6},{6,4},{8,10},{10,8},{12,14},{14,12},{16,18},{18,... | collective-permute-start | bytes 1425416 | tf_op jit(solution)/shard_map/ppermute | solution.py:205
  47.0 14.1 %collective-permute-start.6 = (bf16[256,512]{1,0:T(8,128)(2,1)S(1)}, bf16[256,512]{1,0:T(8,128)(2,1)S(1)}, u32[]{:S(2)}, u32[]{:S(2)}) collective-permute-start(bf16[256,512]{1,0:T(8,128)(2,1)S(1)} %shard_map.126.refs_6_.refs_0_), channel_id=1, source_target_pairs={{0,1},{1,0},{2,3},{3,2},{4,5},{5,4},{6,7},{7,6},{8,9},{9,8},{10,11... | collective-permute-start | bytes 786440 | tf_op jit(solution)/shard_map/ppermute | solution.py:201
  51.5 15.4 %collective-permute-start.13 = (bf16[2,256,512]{2,1,0:T(8,128)(2,1)S(1)}, bf16[2,256,512]{2,1,0:T(8,128)(2,1)S(1)}, u32[]{:S(2)}, u32[]{:S(2)}) collective-permute-start(bf16[2,256,512]{2,1,0:T(8,128)(2,1)S(1)} %shard_map.127.refs_7_), channel_id=1, source_target_pairs={{0,1},{1,0},{2,3},{3,2},{4,5},{5,4},{6,7},{7,6},{8,9},{9,8},{10,11... | collective-permute-start | bytes 1572872 | tf_op jit(solution)/shard_map/ppermute | solution.py:201
  52.9 12.6 %collective-permute-start.12 = (bf16[64,3712]{1,0:T(8,128)(2,1)S(1)}, bf16[64,3712]{1,0:T(8,128)(2,1)S(1)}, u32[]{:S(2)}, u32[]{:S(2)}) collective-permute-start(bf16[64,3712]{1,0:T(8,128)(2,1)S(1)} %collective-permute-done.9.refs_7_.refs_0_.refs_3_), channel_id=1, source_target_pairs={{0,4},{2,6},{4,0},{6,2},{8,12},{10,14},{12,8},{14,10},{16,20},{18,... | collective-permute-start | bytes 1425416 | tf_op jit(solution)/shard_map/ppermute | solution.py:205
  53.4 16.6 %collective-permute-start.14 = (bf16[64,3712]{1,0:T(8,128)(2,1)S(1)}, bf16[64,3712]{1,0:T(8,128)(2,1)S(1)}, u32[]{:S(2)}, u32[]{:S(2)}) collective-permute-start(bf16[64,3712]{1,0:T(8,128)(2,1)S(1)} %shard_map.122.refs_2_.refs_0_.refs_3_), channel_id=1, source_target_pairs={{0,8},{2,10},{4,12},{6,14},{8,0},{10,2},{12,4},{14,6},{16,24},{18,... | collective-permute-start | bytes 1425416 | tf_op jit(solution)/shard_map/ppermute | solution.py:205
  63.9 8.3 %collective-permute-start.15 = (bf16[64,3712]{1,0:T(8,128)(2,1)S(1)}, bf16[64,3712]{1,0:T(8,128)(2,1)S(1)}, u32[]{:S(2)}, u32[]{:S(2)}) collective-permute-start(bf16[64,3712]{1,0:T(8,128)(2,1)S(1)} %collective-permute-done.9.refs_7_.refs_0_.refs_3_), channel_id=1, source_target_pairs={{0,2},{2,0},{4,6},{6,4},{8,10},{10,8},{12,14},{14,12},{16,18},{18,... | collective-permute-start | bytes 1425416 | tf_op jit(solution)/shard_map/ppermute | solution.py:205
  70.1 13.3 %collective-permute-start.19 = (bf16[64,3712]{1,0:T(8,128)(2,1)S(1)}, bf16[64,3712]{1,0:T(8,128)(2,1)S(1)}, u32[]{:S(2)}, u32[]{:S(2)}) collective-permute-start(bf16[64,3712]{1,0:T(8,128)(2,1)S(1)} %collective-permute-done.14.refs_8_.refs_0_.refs_3_), channel_id=1, source_target_pairs={{0,4},{2,6},{4,0},{6,2},{8,12},{10,14},{12,8},{14,10},{16,20},{18,... | collective-permute-start | bytes 1425416 | tf_op jit(solution)/shard_map/ppermute | solution.py:205
  70.6 9.1 %collective-permute-start.18 = (bf16[256,512]{1,0:T(8,128)(2,1)S(1)}, bf16[256,512]{1,0:T(8,128)(2,1)S(1)}, u32[]{:S(2)}, u32[]{:S(2)}) collective-permute-start(bf16[256,512]{1,0:T(8,128)(2,1)S(1)} %shard_map.129.refs_6_.refs_0_), channel_id=1, source_target_pairs={{0,1},{1,0},{2,3},{3,2},{4,5},{5,4},{6,7},{7,6},{8,9},{9,8},{10,11... | collective-permute-start | bytes 786440 | tf_op jit(solution)/shard_map/ppermute | solution.py:201
  74.8 15.4 %collective-permute-start.17 = (bf16[2,256,512]{2,1,0:T(8,128)(2,1)S(1)}, bf16[2,256,512]{2,1,0:T(8,128)(2,1)S(1)}, u32[]{:S(2)}, u32[]{:S(2)}) collective-permute-start(bf16[2,256,512]{2,1,0:T(8,128)(2,1)S(1)} %shard_map.130.refs_7_), channel_id=1, source_target_pairs={{0,1},{1,0},{2,3},{3,2},{4,5},{5,4},{6,7},{7,6},{8,9},{9,8},{10,11... | collective-permute-start | bytes 1572872 | tf_op jit(solution)/shard_map/ppermute | solution.py:201
  86.4 10.4 %collective-permute-start.22 = (bf16[64,3712]{1,0:T(8,128)(2,1)S(1)}, bf16[64,3712]{1,0:T(8,128)(2,1)S(1)}, u32[]{:S(2)}, u32[]{:S(2)}) collective-permute-start(bf16[64,3712]{1,0:T(8,128)(2,1)S(1)} %collective-permute-done.14.refs_8_.refs_0_.refs_3_), channel_id=1, source_target_pairs={{0,2},{2,0},{4,6},{6,4},{8,10},{10,8},{12,14},{14,12},{16,18},{18,... | collective-permute-start | bytes 1425416 | tf_op jit(solution)/shard_map/ppermute | solution.py:205
  93.2 13.4 %collective-permute-start.24 = (bf16[64,3584]{1,0:T(8,128)(2,1)S(1)}, bf16[64,3584]{1,0:T(8,128)(2,1)S(1)}, u32[]{:S(2)}, u32[]{:S(2)}) collective-permute-start(bf16[64,3584]{1,0:T(8,128)(2,1)S(1)} %get-tuple-element.57), channel_id=1, source_target_pairs={{0,2},{2,0},{4,6},{6,4},{8,10},{10,8},{12,14},{14,12},{16,18},{18,... | collective-permute-start | bytes 1376264 | tf_op jit(solution)/shard_map/ppermute | solution.py:205
  93.7 12.9 %collective-permute-start.25 = (bf16[64,3584]{1,0:T(8,128)(2,1)S(1)}, bf16[64,3584]{1,0:T(8,128)(2,1)S(1)}, u32[]{:S(2)}, u32[]{:S(2)}) collective-permute-start(bf16[64,3584]{1,0:T(8,128)(2,1)S(1)} %add_convert_fusion.7.refs_7_), channel_id=1, source_target_pairs={{0,4},{2,6},{4,0},{6,2},{8,12},{10,14},{12,8},{14,10},{16,20},{18,... | collective-permute-start | bytes 1376264 | tf_op jit(solution)/shard_map/ppermute | solution.py:205
  95.2 8.6 %collective-permute-start.20 = (bf16[256,512]{1,0:T(8,128)(2,1)S(1)}, bf16[256,512]{1,0:T(8,128)(2,1)S(1)}, u32[]{:S(2)}, u32[]{:S(2)}) collective-permute-start(bf16[256,512]{1,0:T(8,128)(2,1)S(1)} %shard_map.132.refs_6_.refs_0_), channel_id=1, source_target_pairs={{0,1},{1,0},{2,3},{3,2},{4,5},{5,4},{6,7},{7,6},{8,9},{9,8},{10,11... | collective-permute-start | bytes 786440 | tf_op jit(solution)/shard_map/ppermute | solution.py:201
  96.7 32.6 %collective-permute-start.10 = (bf16[64,3584]{1,0:T(8,128)(2,1)S(1)}, bf16[64,3584]{1,0:T(8,128)(2,1)S(1)}, u32[]{:S(2)}, u32[]{:S(2)}) collective-permute-start(bf16[64,3584]{1,0:T(8,128)(2,1)S(1)} %get-tuple-element.45), channel_id=1, source_target_pairs={{0,2},{2,0},{4,6},{6,4},{8,10},{10,8},{12,14},{14,12},{16,18},{18,... | collective-permute-start | bytes 1376264 | tf_op jit(solution)/shard_map/ppermute | solution.py:205
  99.5 15.0 %collective-permute-start.27 = (bf16[2,256,512]{2,1,0:T(8,128)(2,1)S(1)}, bf16[2,256,512]{2,1,0:T(8,128)(2,1)S(1)}, u32[]{:S(2)}, u32[]{:S(2)}) collective-permute-start(bf16[2,256,512]{2,1,0:T(8,128)(2,1)S(1)} %shard_map.133.refs_7_), channel_id=1, source_target_pairs={{0,1},{1,0},{2,3},{3,2},{4,5},{5,4},{6,7},{7,6},{8,9},{9,8},{10,11... | collective-permute-start | bytes 1572872 | tf_op jit(solution)/shard_map/ppermute | solution.py:201
  106.5 10.7 %collective-permute-start.29 = (bf16[64,3584]{1,0:T(8,128)(2,1)S(1)}, bf16[64,3584]{1,0:T(8,128)(2,1)S(1)}, u32[]{:S(2)}, u32[]{:S(2)}) collective-permute-start(bf16[64,3584]{1,0:T(8,128)(2,1)S(1)} %get-tuple-element.55.refs_7_), channel_id=1, source_target_pairs={{0,2},{2,0},{4,6},{6,4},{8,10},{10,8},{12,14},{14,12},{16,18},{18,... | collective-permute-start | bytes 1376264 | tf_op jit(solution)/shard_map/ppermute | solution.py:205
  106.8 26.0 %collective-permute-start.30 = (bf16[64,3584]{1,0:T(8,128)(2,1)S(1)}, bf16[64,3584]{1,0:T(8,128)(2,1)S(1)}, u32[]{:S(2)}, u32[]{:S(2)}) collective-permute-start(bf16[64,3584]{1,0:T(8,128)(2,1)S(1)} %add_convert_fusion.6.refs_8_), channel_id=1, source_target_pairs={{0,16},{2,18},{4,20},{6,22},{8,24},{10,26},{12,28},{14,30},{16,0},... | collective-permute-start | bytes 1376264 | tf_op jit(solution)/shard_map/ppermute | solution.py:205
  111.9 17.5 %collective-permute-start.26 = (bf16[64,3584]{1,0:T(8,128)(2,1)S(1)}, bf16[64,3584]{1,0:T(8,128)(2,1)S(1)}, u32[]{:S(2)}, u32[]{:S(2)}) collective-permute-start(bf16[64,3584]{1,0:T(8,128)(2,1)S(1)} %add_convert_fusion.5.refs_9_), channel_id=1, source_target_pairs={{0,4},{2,6},{4,0},{6,2},{8,12},{10,14},{12,8},{14,10},{16,20},{18,... | collective-permute-start | bytes 1376264 | tf_op jit(solution)/shard_map/ppermute | solution.py:205
  114.5 20.1 %collective-permute-start.31 = (bf16[64,3584]{1,0:T(8,128)(2,1)S(1)}, bf16[64,3584]{1,0:T(8,128)(2,1)S(1)}, u32[]{:S(2)}, u32[]{:S(2)}) collective-permute-start(bf16[64,3584]{1,0:T(8,128)(2,1)S(1)} %get-tuple-element.67), channel_id=1, source_target_pairs={{0,2},{2,0},{4,6},{6,4},{8,10},{10,8},{12,14},{14,12},{16,18},{18,... | collective-permute-start | bytes 1376264 | tf_op jit(solution)/shard_map/ppermute | solution.py:205
  117.3 8.8 %collective-permute-start.28 = (bf16[256,512]{1,0:T(8,128)(2,1)S(1)}, bf16[256,512]{1,0:T(8,128)(2,1)S(1)}, u32[]{:S(2)}, u32[]{:S(2)}) collective-permute-start(bf16[256,512]{1,0:T(8,128)(2,1)S(1)} %shard_map.135.refs_0_.refs_7_), channel_id=1, source_target_pairs={{0,1},{1,0},{2,3},{3,2},{4,5},{5,4},{6,7},{7,6},{8,9},{9,8},{10,11... | collective-permute-start | bytes 786440 | tf_op jit(solution)/shard_map/ppermute | solution.py:201
  126.1 13.4 %collective-permute-start.32 = (bf16[64,3584]{1,0:T(8,128)(2,1)S(1)}, bf16[64,3584]{1,0:T(8,128)(2,1)S(1)}, u32[]{:S(2)}, u32[]{:S(2)}) collective-permute-start(bf16[64,3584]{1,0:T(8,128)(2,1)S(1)} %add_convert_fusion.4.refs_8_), channel_id=1, source_target_pairs={{0,4},{2,6},{4,0},{6,2},{8,12},{10,14},{12,8},{14,10},{16,20},{18,... | collective-permute-start | bytes 1376264 | tf_op jit(solution)/shard_map/ppermute | solution.py:205
  129.4 14.6 %collective-permute-start.35 = (bf16[64,3584]{1,0:T(8,128)(2,1)S(1)}, bf16[64,3584]{1,0:T(8,128)(2,1)S(1)}, u32[]{:S(2)}, u32[]{:S(2)}) collective-permute-start(bf16[64,3584]{1,0:T(8,128)(2,1)S(1)} %get-tuple-element.73), channel_id=1, source_target_pairs={{0,2},{2,0},{4,6},{6,4},{8,10},{10,8},{12,14},{14,12},{16,18},{18,... | collective-permute-start | bytes 1376264 | tf_op jit(solution)/shard_map/ppermute | solution.py:205
  133.1 15.0 %collective-permute-start.36 = (bf16[64,3584]{1,0:T(8,128)(2,1)S(1)}, bf16[64,3584]{1,0:T(8,128)(2,1)S(1)}, u32[]{:S(2)}, u32[]{:S(2)}) collective-permute-start(bf16[64,3584]{1,0:T(8,128)(2,1)S(1)} %add_convert_fusion.3), channel_id=1, source_target_pairs={{0,4},{2,6},{4,0},{6,2},{8,12},{10,14},{12,8},{14,10},{16,20},{18,... | collective-permute-start | bytes 1376264 | tf_op jit(solution)/shard_map/ppermute | solution.py:205
  139.7 12.9 %collective-permute-start.34 = (bf16[64,3584]{1,0:T(8,128)(2,1)S(1)}, bf16[64,3584]{1,0:T(8,128)(2,1)S(1)}, u32[]{:S(2)}, u32[]{:S(2)}) collective-permute-start(bf16[64,3584]{1,0:T(8,128)(2,1)S(1)} %add_convert_fusion.2), channel_id=1, source_target_pairs={{0,24},{2,26},{4,28},{6,30},{8,16},{10,18},{12,20},{14,22},{16,8},... | collective-permute-start | bytes 1376264 | tf_op jit(solution)/shard_map/ppermute | solution.py:205
  148.2 14.0 %collective-permute-start.37 = (bf16[64,3584]{1,0:T(8,128)(2,1)S(1)}, bf16[64,3584]{1,0:T(8,128)(2,1)S(1)}, u32[]{:S(2)}, u32[]{:S(2)}) collective-permute-start(bf16[64,3584]{1,0:T(8,128)(2,1)S(1)} %add_convert_fusion.1), channel_id=1, source_target_pairs={{0,8},{2,10},{4,12},{6,14},{8,0},{10,2},{12,4},{14,6},{16,24},{18,... | collective-permute-start | bytes 1376264 | tf_op jit(solution)/shard_map/ppermute | solution.py:205
  (6 other events, 24.2 us)
where the time goes:
time: 163 us
  waiting for transfers between devices  62.6 us (38%)
  starting transfers between devices  51.1 us (31%)
  Pallas kernels  42.6 us (26%)
  other arithmetic  3.76 us (2%)
    ppermute x30, waiting for transfers between devices, flipped(): return lax.ppermute(value, 'ep', [(i, i ^ bits) for i in range(size)])  42.3 us
    ppermute x30, starting transfers between devices, flipped(): return lax.ppermute(value, 'ep', [(i, i ^ bits) for i in range(size)])  40.2 us
    pallas_call x8, Pallas kernels, sums(): pl.pallas_call(functools.partial(sums_kernel, len(blocks), len(arrived),...  21.9 us
    ppermute x8, waiting for transfers between devices, shifted(): lax.ppermute(value, axis, [(i, (i + step) % size) for i in range(size)])  20.2 us
    pallas_call x4, Pallas kernels, down_rows(): pl.pallas_call(functools.partial(down_kernel, parts, len(blocks), len(aft...  11.1 us
    ppermute x8, starting transfers between devices, shifted(): lax.ppermute(value, axis, [(i, (i + step) % size) for i in range(size)])  10.9 us
    pallas_call x2, Pallas kernels, load(): pl.pallas_call(lambda *refs: load_kernel(count, *refs[:count], *refs[coun...  8.29 us
  transfers between devices with their start and end apart: 38, of which 16 were waited for; matrix products, arithmetic and copies ran while one was open for 3% of the time, Pallas kernels for 24%

commit v1 on v0

--- a/solution.py
+++ b/solution.py
@@ -14,6 +14,7 @@
 BF16 = jnp.bfloat16
 EXTRA = 128
 PIECES = 3
+PIECES_SENT = (2, 1, 1, 1)
 
 
 def scale_of(extra, step_rows, one, two):
@@ -61,13 +62,14 @@
     )(*[in_hbm(array) for array in arrays], *after)
 
 
-def sums_kernel(block_count, arrived_count, after_count, part, scalar_ref, *refs):
+def sums_kernel(block_count, arrived_count, after_count, part, pieces, scalar_ref, *refs):
     block_refs = refs[:block_count]
     gate_ref, up_ref = refs[block_count : block_count + 2]
     arrived_refs = refs[block_count + 2 : block_count + 2 + arrived_count]
-    out_ref, rows = refs[block_count + 2 + arrived_count + after_count :]
+    out_refs = refs[block_count + 2 + arrived_count + after_count : -1]
+    rows = refs[-1]
     depth = rows.shape[1]
-    part_width = out_ref.shape[-1]
+    part_width = out_refs[0].shape[-1]
     tile = 256 if part_width % 256 == 0 else part_width
     start = 0
     for ref in block_refs:
@@ -79,34 +81,35 @@
         gate = jnp.dot(rows[...], gate_ref[0, :, span], preferred_element_type=F32)
         up = jnp.dot(rows[...], up_ref[0, :, span], preferred_element_type=F32)
         if arrived_count == 0:
-            out_ref[0, :, here] = gate.astype(BF16)
-            out_ref[1, :, here] = up.astype(BF16)
+            out_refs[0][0, :, here] = gate.astype(BF16)
+            out_refs[-1][2 // pieces - 1, :, here] = up.astype(BF16)
         else:
-            for ref in arrived_refs:
-                gate = gate + ref[0, :, here].astype(F32)
-                up = up + ref[1, :, here].astype(F32)
-            out_ref[:, here] = (gate / (1.0 + jnp.exp(-gate)) * up).astype(BF16)
-
-
-def sums(blocks, gate_weight, up_weight, scalars, part, part_width, arrived, after):
+            for gate_in, up_in in zip(arrived_refs[::pieces], arrived_refs[pieces - 1 :: pieces]):
+                gate = gate + gate_in[0, :, here].astype(F32)
+                up = up + up_in[2 // pieces - 1, :, here].astype(F32)
+            out_refs[0][:, here] = (gate / (1.0 + jnp.exp(-gate)) * up).astype(BF16)
+
+
+def sums(blocks, gate_weight, up_weight, scalars, part, part_width, pieces, arrived, after):
     count = sum(block.shape[0] for block in blocks)
     depth = gate_weight.shape[1]
-    out_shape = (count, part_width) if arrived else (2, count, part_width)
+    outs = 1 if arrived else pieces
+    out_shape = (count, part_width) if arrived else (2 // pieces, count, part_width)
     any_spec = pl.BlockSpec(memory_space=pl.ANY)
     vmem_spec = pl.BlockSpec(memory_space=pltpu.VMEM)
     return pl.pallas_call(
-        functools.partial(sums_kernel, len(blocks), len(arrived), len(after), part),
-        out_shape=jax.ShapeDtypeStruct(out_shape, BF16),
+        functools.partial(sums_kernel, len(blocks), len(arrived), len(after), part, pieces),
+        out_shape=[jax.ShapeDtypeStruct(out_shape, BF16)] * outs,
         grid_spec=pltpu.PrefetchScalarGridSpec(
             num_scalar_prefetch=1,
             grid=(),
             in_specs=[vmem_spec] * (len(blocks) + 2 + len(arrived)) + [any_spec] * len(after),
-            out_specs=vmem_spec,
+            out_specs=[vmem_spec] * outs,
             scratch_shapes=[pltpu.VMEM((count, depth), BF16)],
         ),
         compiler_params=pltpu.CompilerParams(
             vmem_limit_bytes=vmem_limit(
-                (count, depth), *[block.shape for block in blocks], *[pair.shape for pair in arrived], out_shape
+                (count, depth), *[block.shape for block in blocks], *[pair.shape for pair in arrived], *[out_shape] * outs
             )
         ),
         cost_estimate=QUICK,
@@ -270,6 +273,9 @@
     def hold_x(g):
         last.extend(state[g]["across"])
 
+    def hold_blocks(g):
+        last.extend(state[g]["blocks"])
+
     def hold_core(g):
         last.append(state[g]["core_far"])
 
@@ -277,14 +283,14 @@
         state[g]["arrived"] = []
         for step in range(1, rep):
             partial = sums(
-                state[g]["blocks"], gate_weight, up_weight, scalars, 1 + rep + step, part_width, [], last
+                state[g]["blocks"], gate_weight, up_weight, scalars, 1 + rep + step, part_width, PIECES_SENT[g], [], last
             )
-            last[:] = [partial]
-            state[g]["arrived"].append(shifted(partial, "rep", rep, step))
+            last[:] = [partial[-1]]
+            state[g]["arrived"] += [shifted(value, "rep", rep, step) for value in partial]
 
     def send_hidden(g):
-        hidden = sums(
-            state[g]["blocks"], gate_weight, up_weight, scalars, 2, part_width, state[g]["arrived"], last
+        (hidden,) = sums(
+            state[g]["blocks"], gate_weight, up_weight, scalars, 2, part_width, PIECES_SENT[g], state[g]["arrived"], last
         )
         last[:] = [hidden]
         state[g]["hidden"] = [hidden] + [shifted(hidden, "rep", rep, step) for step in range(1, rep)]
@@ -331,8 +337,8 @@
         for stage, g in turns:
             stage(g)
 
-    run((ask_x, 0), (ask_core, 0), (hold_z, 1), (send_sums, 0), (ask_x, 1), (hold_x, 1), (send_hidden, 0), (ask_core, 1))
-    run((hold_z, 2), (send_sums, 1), (ask_x, 2), (send_core, 0), (hold_x, 2), (send_hidden, 1), (hold_core, 0), (hold_z, 3))
+    run((ask_x, 0), (hold_z, 1), (ask_core, 0), (ask_x, 1), (send_sums, 0), (hold_x, 1), (send_hidden, 0), (hold_z, 2), (ask_core, 1))
+    run((send_sums, 1), (ask_x, 2), (send_core, 0), (hold_x, 2), (send_hidden, 1), (hold_core, 0), (hold_z, 3))
     run((ask_core, 2), (ask_x, 3), (send_sums, 2), (hold_x, 3), (send_core, 1), (send_hidden, 2), (send_x, 1))
     run((ask_core, 3), (send_sums, 3), (send_core, 2), (send_z, 1), (send_x, 0), (send_hidden, 3), (send_x, 2))
     run((send_core, 3), (send_z, 0), (finish, 0), (finish, 1), (send_x, 3), (send_z, 2), (send_z, 3), (finish, 2), (finish, 3))

time: 163 us -> 167 us (1.025)
  waiting for transfers between devices: 62.6 us -> 83 us
  starting transfers between devices: 51.1 us -> 34.2 us
    ppermute x30, starting transfers between devices: 40.2 us -> 22.5 us  [flipped(): return lax.ppermute(value, 'ep', [(i, i ^ bits) for i in range(size)])]
    ppermute x8 -> x9, waiting for transfers between devices: 20.2 us -> 34.5 us  [shifted(): lax.ppermute(value, axis, [(i, (i + step) % size) for i in range(size)])]
    ppermute x30, waiting for transfers between devices: 42.3 us -> 48.4 us  [flipped(): return lax.ppermute(value, 'ep', [(i, i ^ bits) for i in range(size)])]
    ppermute x8 -> x9, starting transfers between devices: 10.9 us -> 11.7 us  [shifted(): lax.ppermute(value, axis, [(i, (i + step) % size) for i in range(size)])]
  transfers between devices with their start and end apart: 38 -> 39, of which waited for: 16 -> 20; matrix products, arithmetic and copies ran while one was open for 3% -> 3% of each run, Pallas kernels for 24% -> 25%
where the time goes in v1:
time: 167 us
  waiting for transfers between devices  83 us (50%)
  Pallas kernels  42.6 us (26%)
  starting transfers between devices  34.2 us (20%)
  other arithmetic  3.78 us (2%)
    ppermute x30, waiting for transfers between devices, flipped(): return lax.ppermute(value, 'ep', [(i, i ^ bits) for i in range(size)])  48.4 us
    ppermute x9, waiting for transfers between devices, shifted(): lax.ppermute(value, axis, [(i, (i + step) % size) for i in range(size)])  34.5 us
    ppermute x30, starting transfers between devices, flipped(): return lax.ppermute(value, 'ep', [(i, i ^ bits) for i in range(size)])  22.5 us
    pallas_call x8, Pallas kernels, sums(): pl.pallas_call(functools.partial(sums_kernel, len(blocks), len(arrived),...  21.9 us
    ppermute x9, starting transfers between devices, shifted(): lax.ppermute(value, axis, [(i, (i + step) % size) for i in range(size)])  11.7 us
    pallas_call x4, Pallas kernels, down_rows(): pl.pallas_call(functools.partial(down_kernel, parts, len(blocks), len(aft...  11.1 us
    pallas_call x2, Pallas kernels, load(): pl.pallas_call(lambda *refs: load_kernel(count, *refs[:count], *refs[coun...  8.29 us
  transfers between devices with their start and end apart: 39, of which 20 were waited for; matrix products, arithmetic and copies ran while one was open for 3% of the time, Pallas kernels for 25%

profile of v1, /device:TPU:0, one launch (start us, length us, event | category | flops | bytes accessed | tf_op | source)
XLA Modules:
  0.0 166.7 jit_solution(14156730237319551799)
XLA Ops:
  1.9 4.1 %collective-permute-start.1 = (bf16[64,3712]{1,0:T(8,128)(2,1)S(1)}, bf16[64,3712]{1,0:T(8,128)(2,1)S(1)}, u32[]{:S(2)}, u32[]{:S(2)}) collective-permute-start(bf16[64,3712]{1,0:T(8,128)(2,1)S(1)} %shard_map.122.refs_2_.refs_0_.refs_3_), channel_id=1, source_target_pairs={{0,16},{2,18},{4,20},{6,22},{8,24},{10,26},{12,28},{14,30},{16,0},... | collective-permute-start | bytes 1425416 | tf_op jit(solution)/shard_map/ppermute | solution.py:208
  11.5 5.2 %shard_map.123 = (bf16[1,3584,1024]{2,1,0:T(8,128)(2,1)S(1)}, bf16[1,3584,1024]{2,1,0:T(8,128)(2,1)S(1)}) custom-call(bf16[1,3584,1024]{2,1,0:T(8,128)(2,1)} %refs_0_.2, bf16[1,3584,1024]{2,1,0:T(8,128)(2,1)} %refs_1_.1, bf16[64,3712]{1,0:T(8,128)(2,1)S(1)} %shard_map.122.refs_2_.refs_0_.refs_3_, s32[5]{0:T(128)S(1)} %stack.23.refs_3_.scalar_ref), custom_call_target="tpu_custom_call" | custom-call | flops 1 | bytes 1 | tf_op jit(solution)/shard_map/pallas_call | solution.py:54
  16.7 3.1 %shard_map.124.refs_6_.refs_2_ = bf16[1,1024,3584]{2,1,0:T(8,128)(2,1)S(1)} custom-call(bf16[1,1024,3584]{2,1,0:T(8,128)(2,1)} %refs_0_.3, bf16[1,3584,1024]{2,1,0:T(8,128)(2,1)S(1)} %get-tuple-element.41.refs_1_.refs_4_), custom_call_target="tpu_custom_call" | custom-call | flops 1 | bytes 1 | tf_op jit(solution)/shard_map/pallas_call | solution.py:54
  19.8 7.3 %collective-permute-done.1.refs_7_.refs_0_.refs_3_ = bf16[64,3712]{1,0:T(8,128)(2,1)S(1)} collective-permute-done((bf16[64,3712]{1,0:T(8,128)(2,1)S(1)}, bf16[64,3712]{1,0:T(8,128)(2,1)S(1)}, u32[]{:S(2)}, u32[]{:S(2)}) %collective-permute-start.1) | collective-permute-done | bytes 475168 | tf_op jit(solution)/shard_map/ppermute | solution.py:208
  28.6 3.5 %collective-permute-start.8 = (bf16[64,3712]{1,0:T(8,128)(2,1)S(1)}, bf16[64,3712]{1,0:T(8,128)(2,1)S(1)}, u32[]{:S(2)}, u32[]{:S(2)}) collective-permute-start(bf16[64,3712]{1,0:T(8,128)(2,1)S(1)} %shard_map.122.refs_2_.refs_0_.refs_3_), channel_id=1, source_target_pairs={{0,24},{2,26},{4,28},{6,30},{8,16},{10,18},{12,20},{14,22},{16,8},... | collective-permute-start | bytes 1425416 | tf_op jit(solution)/shard_map/ppermute | solution.py:208
  32.2 2.7 %shard_map.125 = (bf16[1,256,512]{2,1,0:T(8,128)(2,1)S(1)}, bf16[1,256,512]{2,1,0:T(8,128)(2,1)S(1)}) custom-call(s32[5]{0:T(128)S(1)} %stack.23.refs_3_.scalar_ref, bf16[64,3712]{1,0:T(8,128)(2,1)S(1)} %shard_map.122.refs_2_.refs_0_.refs_3_, bf16[64,3712]{1,0:T(8,128)(2,1)S(1)} %collective-permute-done.refs_1_.refs_4_, ...), custom_call_target="tpu_custom_call" | custom-call | flops 1 | bytes 1 | tf_op jit(solution)/shard_map/pallas_call | solution.py:100
  34.8 1.6 collective-permute-start.4
  36.9 3.5 %collective-permute-done.6.refs_9_.refs_1_.refs_4_ = bf16[64,3712]{1,0:T(8,128)(2,1)S(1)} collective-permute-done((bf16[64,3712]{1,0:T(8,128)(2,1)S(1)}, bf16[64,3712]{1,0:T(8,128)(2,1)S(1)}, u32[]{:S(2)}, u32[]{:S(2)}) %collective-permute-start.6) | collective-permute-done | bytes 475168 | tf_op jit(solution)/shard_map/ppermute | solution.py:208
  40.4 3.7 %collective-permute-done.4.refs_6_ = bf16[1,256,512]{2,1,0:T(8,128)(2,1)S(1)} collective-permute-done((bf16[1,256,512]{2,1,0:T(8,128)(2,1)S(1)}, bf16[1,256,512]{2,1,0:T(8,128)(2,1)S(1)}, u32[]{:S(2)}, u32[]{:S(2)}) %collective-permute-start.4) | collective-permute-done | bytes 262176 | tf_op jit(solution)/shard_map/ppermute | solution.py:204
  44.1 4.6 %collective-permute-done.5.refs_7_ = bf16[1,256,512]{2,1,0:T(8,128)(2,1)S(1)} collective-permute-done((bf16[1,256,512]{2,1,0:T(8,128)(2,1)S(1)}, bf16[1,256,512]{2,1,0:T(8,128)(2,1)S(1)}, u32[]{:S(2)}, u32[]{:S(2)}) %collective-permute-start.5) | collective-permute-done | bytes 262176 | tf_op jit(solution)/shard_map/ppermute | solution.py:204
  48.7 2.8 %shard_map.126.refs_6_.refs_0_ = bf16[256,512]{1,0:T(8,128)(2,1)S(1)} custom-call(s32[5]{0:T(128)S(1)} %stack.23.refs_3_.scalar_ref, bf16[64,3712]{1,0:T(8,128)(2,1)S(1)} %shard_map.122.refs_2_.refs_0_.refs_3_, bf16[64,3712]{1,0:T(8,128)(2,1)S(1)} %collective-permute-done.refs_1_.refs_4_, bf16[64,3712]{1,0:T(8,128)(2,1)S(1)} %collective-permute-done.2.refs_2_.refs_5_, ...), custom_call_target="tpu_custom_call" | custom-call | flops 1 | bytes 1 | tf_op jit(solution)/shard_map/pallas_call | solution.py:100
  53.3 2.7 %shard_map.127.refs_7_ = bf16[2,256,512]{2,1,0:T(8,128)(2,1)S(1)} custom-call(s32[5]{0:T(128)S(1)} %stack.23.refs_3_.scalar_ref, bf16[64,3712]{1,0:T(8,128)(2,1)S(1)} %collective-permute-done.1.refs_7_.refs_0_.refs_3_, bf16[64,3712]{1,0:T(8,128)(2,1)S(1)} %collective-permute-done.6.refs_9_.refs_1_.refs_4_, ...), custom_call_target="tpu_custom_call" | custom-call | flops 1 | bytes 1 | tf_op jit(solution)/shard_map/pallas_call | solution.py:100
  60.7 2.7 %shard_map.128 = (f32[64,3584]{1,0:T(8,128)S(1)}, f32[64,3584]{1,0:T(8,128)S(1)}, bf16[64,3584]{1,0:T(8,128)(2,1)S(1)}, bf16[64,3584]{1,0:T(8,128)(2,1)S(1)}) custom-call(s32[5]{0:T(128)S(1)} %stack.23.refs_3_.scalar_ref, bf16[256,512]{1,0:T(8,128)(2,1)S(1)} %shard_map.126.refs_6_.refs_0_, bf16[256,512]{1,0:T(8,128)(2,1)S(1)} %collective-permute-done.7.refs_1_, ...), custom_call_target="tpu_custom_call" | custom-call | flops 1 | bytes 1 | tf_op jit(solution)/shard_map/pallas_call | solution.py:147
  64.0 6.3 %collective-permute-done.13.refs_8_.refs_1_.refs_4_ = bf16[64,3712]{1,0:T(8,128)(2,1)S(1)} collective-permute-done((bf16[64,3712]{1,0:T(8,128)(2,1)S(1)}, bf16[64,3712]{1,0:T(8,128)(2,1)S(1)}, u32[]{:S(2)}, u32[]{:S(2)}) %collective-permute-start.13) | collective-permute-done | bytes 475168 | tf_op jit(solution)/shard_map/ppermute | solution.py:208
  71.5 2.8 %shard_map.129.refs_6_.refs_0_ = bf16[256,512]{1,0:T(8,128)(2,1)S(1)} custom-call(s32[5]{0:T(128)S(1)} %stack.23.refs_3_.scalar_ref, bf16[64,3712]{1,0:T(8,128)(2,1)S(1)} %collective-permute-done.1.refs_7_.refs_0_.refs_3_, bf16[64,3712]{1,0:T(8,128)(2,1)S(1)} %collective-permute-done.6.refs_9_.refs_1_.refs_4_, ...), custom_call_target="tpu_custom_call" | custom-call | flops 1 | bytes 1 | tf_op jit(solution)/shard_map/pallas_call | solution.py:100
  76.5 2.7 %shard_map.130.refs_7_ = bf16[2,256,512]{2,1,0:T(8,128)(2,1)S(1)} custom-call(s32[5]{0:T(128)S(1)} %stack.23.refs_3_.scalar_ref, bf16[64,3712]{1,0:T(8,128)(2,1)S(1)} %collective-permute-done.8.refs_7_.refs_0_.refs_3_, bf16[64,3712]{1,0:T(8,128)(2,1)S(1)} %collective-permute-done.13.refs_8_.refs_1_.refs_4_, ...), custom_call_target="tpu_custom_call" | custom-call | flops 1 | bytes 1 | tf_op jit(solution)/shard_map/pallas_call | solution.py:100
  80.5 3.6 %collective-permute-done.19.refs_1_ = bf16[256,512]{1,0:T(8,128)(2,1)S(1)} collective-permute-done((bf16[256,512]{1,0:T(8,128)(2,1)S(1)}, bf16[256,512]{1,0:T(8,128)(2,1)S(1)}, u32[]{:S(2)}, u32[]{:S(2)}) %collective-permute-start.19) | collective-permute-done | bytes 262176 | tf_op jit(solution)/shard_map/ppermute | solution.py:204
  84.1 3.5 %collective-permute-done.20.refs_8_.refs_1_.refs_4_ = bf16[64,3712]{1,0:T(8,128)(2,1)S(1)} collective-permute-done((bf16[64,3712]{1,0:T(8,128)(2,1)S(1)}, bf16[64,3712]{1,0:T(8,128)(2,1)S(1)}, u32[]{:S(2)}, u32[]{:S(2)}) %collective-permute-start.20) | collective-permute-done | bytes 475168 | tf_op jit(solution)/shard_map/ppermute | solution.py:208
  87.6 2.9 %shard_map.131 = (f32[64,3584]{1,0:T(8,128)S(1)}, f32[64,3584]{1,0:T(8,128)S(1)}, bf16[64,3584]{1,0:T(8,128)(2,1)S(1)}, bf16[64,3584]{1,0:T(8,128)(2,1)S(1)}) custom-call(s32[5]{0:T(128)S(1)} %stack.23.refs_3_.scalar_ref, bf16[256,512]{1,0:T(8,128)(2,1)S(1)} %shard_map.129.refs_6_.refs_0_, bf16[256,512]{1,0:T(8,128)(2,1)S(1)} %collective-permute-done.19.refs_1_, ...), custom_call_target="tpu_custom_call" | custom-call | flops 1 | bytes 1 | tf_op jit(solution)/shard_map/pallas_call | solution.py:147
  91.2 3.4 %collective-permute-done.18.refs_6_ = bf16[2,256,512]{2,1,0:T(8,128)(2,1)S(1)} collective-permute-done((bf16[2,256,512]{2,1,0:T(8,128)(2,1)S(1)}, bf16[2,256,512]{2,1,0:T(8,128)(2,1)S(1)}, u32[]{:S(2)}, u32[]{:S(2)}) %collective-permute-start.18) | collective-permute-done | bytes 524320 | tf_op jit(solution)/shard_map/ppermute | solution.py:204
  94.6 2.8 %shard_map.132.refs_6_.refs_0_ = bf16[256,512]{1,0:T(8,128)(2,1)S(1)} custom-call(s32[5]{0:T(128)S(1)} %stack.23.refs_3_.scalar_ref, bf16[64,3712]{1,0:T(8,128)(2,1)S(1)} %collective-permute-done.8.refs_7_.refs_0_.refs_3_, bf16[64,3712]{1,0:T(8,128)(2,1)S(1)} %collective-permute-done.13.refs_8_.refs_1_.refs_4_, ...), custom_call_target="tpu_custom_call" | custom-call | flops 1 | bytes 1 | tf_op jit(solution)/shard_map/pallas_call | solution.py:100
  101.1 2.7 %shard_map.133.refs_7_ = bf16[2,256,512]{2,1,0:T(8,128)(2,1)S(1)} custom-call(s32[5]{0:T(128)S(1)} %stack.23.refs_3_.scalar_ref, bf16[64,3712]{1,0:T(8,128)(2,1)S(1)} %collective-permute-done.15.refs_8_.refs_0_.refs_3_, bf16[64,3712]{1,0:T(8,128)(2,1)S(1)} %collective-permute-done.20.refs_8_.refs_1_.refs_4_, ...), custom_call_target="tpu_custom_call" | custom-call | flops 1 | bytes 1 | tf_op jit(solution)/shard_map/pallas_call | solution.py:100
  104.3 3.7 %collective-permute-done.21.refs_1_ = bf16[256,512]{1,0:T(8,128)(2,1)S(1)} collective-permute-done((bf16[256,512]{1,0:T(8,128)(2,1)S(1)}, bf16[256,512]{1,0:T(8,128)(2,1)S(1)}, u32[]{:S(2)}, u32[]{:S(2)}) %collective-permute-start.21) | collective-permute-done | bytes 262176 | tf_op jit(solution)/shard_map/ppermute | solution.py:204
  108.1 2.7 %shard_map.134 = (f32[64,3584]{1,0:T(8,128)S(1)}, f32[64,3584]{1,0:T(8,128)S(1)}, bf16[64,3584]{1,0:T(8,128)(2,1)S(1)}, bf16[64,3584]{1,0:T(8,128)(2,1)S(1)}) custom-call(s32[5]{0:T(128)S(1)} %stack.23.refs_3_.scalar_ref, bf16[256,512]{1,0:T(8,128)(2,1)S(1)} %shard_map.132.refs_6_.refs_0_, bf16[256,512]{1,0:T(8,128)(2,1)S(1)} %collective-permute-done.21.refs_1_, ...), custom_call_target="tpu_custom_call" | custom-call | flops 1 | bytes 1 | tf_op jit(solution)/shard_map/pallas_call | solution.py:147
  113.1 5.6 %collective-permute-done.28.refs_6_ = bf16[2,256,512]{2,1,0:T(8,128)(2,1)S(1)} collective-permute-done((bf16[2,256,512]{2,1,0:T(8,128)(2,1)S(1)}, bf16[2,256,512]{2,1,0:T(8,128)(2,1)S(1)}, u32[]{:S(2)}, u32[]{:S(2)}) %collective-permute-start.28) | collective-permute-done | bytes 524320 | tf_op jit(solution)/shard_map/ppermute | solution.py:204
  118.8 2.8 %shard_map.135.refs_0_.refs_7_ = bf16[256,512]{1,0:T(8,128)(2,1)S(1)} custom-call(s32[5]{0:T(128)S(1)} %stack.23.refs_3_.scalar_ref, bf16[64,3712]{1,0:T(8,128)(2,1)S(1)} %collective-permute-done.15.refs_8_.refs_0_.refs_3_, bf16[64,3712]{1,0:T(8,128)(2,1)S(1)} %collective-permute-done.20.refs_8_.refs_1_.refs_4_, ...), custom_call_target="tpu_custom_call" | custom-call | flops 1 | bytes 1 | tf_op jit(solution)/shard_map/pallas_call | solution.py:100
  123.2 7.1 %collective-permute-done.29.refs_1_ = bf16[256,512]{1,0:T(8,128)(2,1)S(1)} collective-permute-done((bf16[256,512]{1,0:T(8,128)(2,1)S(1)}, bf16[256,512]{1,0:T(8,128)(2,1)S(1)}, u32[]{:S(2)}, u32[]{:S(2)}) %collective-permute-start.29) | collective-permute-done | bytes 262176 | tf_op jit(solution)/shard_map/ppermute | solution.py:204
  130.9 2.7 %shard_map.136 = (f32[64,3584]{1,0:T(8,128)S(1)}, f32[64,3584]{1,0:T(8,128)S(1)}, bf16[64,3584]{1,0:T(8,128)(2,1)S(1)}, bf16[64,3584]{1,0:T(8,128)(2,1)S(1)}) custom-call(s32[5]{0:T(128)S(1)} %stack.23.refs_3_.scalar_ref, bf16[256,512]{1,0:T(8,128)(2,1)S(1)} %shard_map.135.refs_0_.refs_7_, bf16[256,512]{1,0:T(8,128)(2,1)S(1)} %collective-permute-done.29.refs_1_, ...), custom_call_target="tpu_custom_call" | custom-call | flops 1 | bytes 1 | tf_op jit(solution)/shard_map/pallas_call | solution.py:147
  137.2 6.6 %collective-permute-done.33 = bf16[64,3584]{1,0:T(8,128)(2,1)S(1)} collective-permute-done((bf16[64,3584]{1,0:T(8,128)(2,1)S(1)}, bf16[64,3584]{1,0:T(8,128)(2,1)S(1)}, u32[]{:S(2)}, u32[]{:S(2)}) %collective-permute-start.33) | collective-permute-done | bytes 458784 | tf_op jit(solution)/shard_map/ppermute | solution.py:208
  144.6 7.7 %collective-permute-done.37 = bf16[64,3584]{1,0:T(8,128)(2,1)S(1)} collective-permute-done((bf16[64,3584]{1,0:T(8,128)(2,1)S(1)}, bf16[64,3584]{1,0:T(8,128)(2,1)S(1)}, u32[]{:S(2)}, u32[]{:S(2)}) %collective-permute-start.37) | collective-permute-done | bytes 458784 | tf_op jit(solution)/shard_map/ppermute | solution.py:208
  153.5 3.9 %collective-permute-done.35 = bf16[64,3584]{1,0:T(8,128)(2,1)S(1)} collective-permute-done((bf16[64,3584]{1,0:T(8,128)(2,1)S(1)}, bf16[64,3584]{1,0:T(8,128)(2,1)S(1)}, u32[]{:S(2)}, u32[]{:S(2)}) %collective-permute-start.35) | collective-permute-done | bytes 458784 | tf_op jit(solution)/shard_map/ppermute | solution.py:208
  157.5 8.3 %collective-permute-done.38 = bf16[64,3584]{1,0:T(8,128)(2,1)S(1)} collective-permute-done((bf16[64,3584]{1,0:T(8,128)(2,1)S(1)}, bf16[64,3584]{1,0:T(8,128)(2,1)S(1)}, u32[]{:S(2)}, u32[]{:S(2)}) %collective-permute-start.38) | collective-permute-done | bytes 458784 | tf_op jit(solution)/shard_map/ppermute | solution.py:208
  (75 shorter events, 35.7 us)
Async XLA Ops:
  1.9 25.2 %collective-permute-start.1 = (bf16[64,3712]{1,0:T(8,128)(2,1)S(1)}, bf16[64,3712]{1,0:T(8,128)(2,1)S(1)}, u32[]{:S(2)}, u32[]{:S(2)}) collective-permute-start(bf16[64,3712]{1,0:T(8,128)(2,1)S(1)} %shard_map.122.refs_2_.refs_0_.refs_3_), channel_id=1, source_target_pairs={{0,16},{2,18},{4,20},{6,22},{8,24},{10,26},{12,28},{14,30},{16,0},... | collective-permute-start | bytes 1425416 | tf_op jit(solution)/shard_map/ppermute | solution.py:208
  6.0 21.1 %collective-permute-start = (bf16[64,3712]{1,0:T(8,128)(2,1)S(1)}, bf16[64,3712]{1,0:T(8,128)(2,1)S(1)}, u32[]{:S(2)}, u32[]{:S(2)}) collective-permute-start(bf16[64,3712]{1,0:T(8,128)(2,1)S(1)} %shard_map.122.refs_2_.refs_0_.refs_3_), channel_id=1, source_target_pairs={{0,4},{2,6},{4,0},{6,2},{8,12},{10,14},{12,8},{14,10},{16,20},{18,... | collective-permute-start | bytes 1425416 | tf_op jit(solution)/shard_map/ppermute | solution.py:208
  7.5 24.6 %collective-permute-start.2 = (bf16[64,3712]{1,0:T(8,128)(2,1)S(1)}, bf16[64,3712]{1,0:T(8,128)(2,1)S(1)}, u32[]{:S(2)}, u32[]{:S(2)}) collective-permute-start(bf16[64,3712]{1,0:T(8,128)(2,1)S(1)} %shard_map.122.refs_2_.refs_0_.refs_3_), channel_id=1, source_target_pairs={{0,2},{2,0},{4,6},{6,4},{8,10},{10,8},{12,14},{14,12},{16,18},{18,... | collective-permute-start | bytes 1425416 | tf_op jit(solution)/shard_map/ppermute | solution.py:208
  27.1 13.3 %collective-permute-start.6 = (bf16[64,3712]{1,0:T(8,128)(2,1)S(1)}, bf16[64,3712]{1,0:T(8,128)(2,1)S(1)}, u32[]{:S(2)}, u32[]{:S(2)}) collective-permute-start(bf16[64,3712]{1,0:T(8,128)(2,1)S(1)} %collective-permute-done.1.refs_7_.refs_0_.refs_3_), channel_id=1, source_target_pairs={{0,4},{2,6},{4,0},{6,2},{8,12},{10,14},{12,8},{14,10},{16,20},{18,... | collective-permute-start | bytes 1425416 | tf_op jit(solution)/shard_map/ppermute | solution.py:208
  28.6 22.8 %collective-permute-start.8 = (bf16[64,3712]{1,0:T(8,128)(2,1)S(1)}, bf16[64,3712]{1,0:T(8,128)(2,1)S(1)}, u32[]{:S(2)}, u32[]{:S(2)}) collective-permute-start(bf16[64,3712]{1,0:T(8,128)(2,1)S(1)} %shard_map.122.refs_2_.refs_0_.refs_3_), channel_id=1, source_target_pairs={{0,24},{2,26},{4,28},{6,30},{8,16},{10,18},{12,20},{14,22},{16,8},... | collective-permute-start | bytes 1425416 | tf_op jit(solution)/shard_map/ppermute | solution.py:208
  34.8 9.2 %collective-permute-start.4 = (bf16[1,256,512]{2,1,0:T(8,128)(2,1)S(1)}, bf16[1,256,512]{2,1,0:T(8,128)(2,1)S(1)}, u32[]{:S(2)}, u32[]{:S(2)}) collective-permute-start(bf16[1,256,512]{2,1,0:T(8,128)(2,1)S(1)} %get-tuple-element.44), channel_id=1, source_target_pairs={{0,1},{1,0},{2,3},{3,2},{4,5},{5,4},{6,7},{7,6},{8,9},{9,8},{10,11... | collective-permute-start | bytes 786440 | tf_op jit(solution)/shard_map/ppermute | solution.py:204
  36.5 12.2 %collective-permute-start.5 = (bf16[1,256,512]{2,1,0:T(8,128)(2,1)S(1)}, bf16[1,256,512]{2,1,0:T(8,128)(2,1)S(1)}, u32[]{:S(2)}, u32[]{:S(2)}) collective-permute-start(bf16[1,256,512]{2,1,0:T(8,128)(2,1)S(1)} %get-tuple-element.45.refs_8_), channel_id=1, source_target_pairs={{0,1},{1,0},{2,3},{3,2},{4,5},{5,4},{6,7},{7,6},{8,9},{9,8},{10,11... | collective-permute-start | bytes 786440 | tf_op jit(solution)/shard_map/ppermute | solution.py:204
  36.9 16.2 %collective-permute-start.9 = (bf16[64,3712]{1,0:T(8,128)(2,1)S(1)}, bf16[64,3712]{1,0:T(8,128)(2,1)S(1)}, u32[]{:S(2)}, u32[]{:S(2)}) collective-permute-start(bf16[64,3712]{1,0:T(8,128)(2,1)S(1)} %collective-permute-done.1.refs_7_.refs_0_.refs_3_), channel_id=1, source_target_pairs={{0,2},{2,0},{4,6},{6,4},{8,10},{10,8},{12,14},{14,12},{16,18},{18,... | collective-permute-start | bytes 1425416 | tf_op jit(solution)/shard_map/ppermute | solution.py:208
  51.5 9.2 %collective-permute-start.7 = (bf16[256,512]{1,0:T(8,128)(2,1)S(1)}, bf16[256,512]{1,0:T(8,128)(2,1)S(1)}, u32[]{:S(2)}, u32[]{:S(2)}) collective-permute-start(bf16[256,512]{1,0:T(8,128)(2,1)S(1)} %shard_map.126.refs_6_.refs_0_), channel_id=1, source_target_pairs={{0,1},{1,0},{2,3},{3,2},{4,5},{5,4},{6,7},{7,6},{8,9},{9,8},{10,11... | collective-permute-start | bytes 786440 | tf_op jit(solution)/shard_map/ppermute | solution.py:204
  56.1 15.4 %collective-permute-start.14 = (bf16[2,256,512]{2,1,0:T(8,128)(2,1)S(1)}, bf16[2,256,512]{2,1,0:T(8,128)(2,1)S(1)}, u32[]{:S(2)}, u32[]{:S(2)}) collective-permute-start(bf16[2,256,512]{2,1,0:T(8,128)(2,1)S(1)} %shard_map.127.refs_7_), channel_id=1, source_target_pairs={{0,1},{1,0},{2,3},{3,2},{4,5},{5,4},{6,7},{7,6},{8,9},{9,8},{10,11... | collective-permute-start | bytes 1572872 | tf_op jit(solution)/shard_map/ppermute | solution.py:204
  57.6 12.6 %collective-permute-start.13 = (bf16[64,3712]{1,0:T(8,128)(2,1)S(1)}, bf16[64,3712]{1,0:T(8,128)(2,1)S(1)}, u32[]{:S(2)}, u32[]{:S(2)}) collective-permute-start(bf16[64,3712]{1,0:T(8,128)(2,1)S(1)} %collective-permute-done.8.refs_7_.refs_0_.refs_3_), channel_id=1, source_target_pairs={{0,4},{2,6},{4,0},{6,2},{8,12},{10,14},{12,8},{14,10},{16,20},{18,... | collective-permute-start | bytes 1425416 | tf_op jit(solution)/shard_map/ppermute | solution.py:208
  58.2 16.1 %collective-permute-start.15 = (bf16[64,3712]{1,0:T(8,128)(2,1)S(1)}, bf16[64,3712]{1,0:T(8,128)(2,1)S(1)}, u32[]{:S(2)}, u32[]{:S(2)}) collective-permute-start(bf16[64,3712]{1,0:T(8,128)(2,1)S(1)} %shard_map.122.refs_2_.refs_0_.refs_3_), channel_id=1, source_target_pairs={{0,8},{2,10},{4,12},{6,14},{8,0},{10,2},{12,4},{14,6},{16,24},{18,... | collective-permute-start | bytes 1425416 | tf_op jit(solution)/shard_map/ppermute | solution.py:208
  63.4 10.8 %collective-permute-start.12 = (bf16[64,3584]{1,0:T(8,128)(2,1)S(1)}, bf16[64,3584]{1,0:T(8,128)(2,1)S(1)}, u32[]{:S(2)}, u32[]{:S(2)}) collective-permute-start(bf16[64,3584]{1,0:T(8,128)(2,1)S(1)} %get-tuple-element.51.refs_7_), channel_id=1, source_target_pairs={{0,2},{2,0},{4,6},{6,4},{8,10},{10,8},{12,14},{14,12},{16,18},{18,... | collective-permute-start | bytes 1376264 | tf_op jit(solution)/shard_map/ppermute | solution.py:208
  63.5 13.0 %collective-permute-start.16 = (bf16[64,3712]{1,0:T(8,128)(2,1)S(1)}, bf16[64,3712]{1,0:T(8,128)(2,1)S(1)}, u32[]{:S(2)}, u32[]{:S(2)}) collective-permute-start(bf16[64,3712]{1,0:T(8,128)(2,1)S(1)} %collective-permute-done.8.refs_7_.refs_0_.refs_3_), channel_id=1, source_target_pairs={{0,2},{2,0},{4,6},{6,4},{8,10},{10,8},{12,14},{14,12},{16,18},{18,... | collective-permute-start | bytes 1425416 | tf_op jit(solution)/shard_map/ppermute | solution.py:208
  74.4 13.3 %collective-permute-start.20 = (bf16[64,3712]{1,0:T(8,128)(2,1)S(1)}, bf16[64,3712]{1,0:T(8,128)(2,1)S(1)}, u32[]{:S(2)}, u32[]{:S(2)}) collective-permute-start(bf16[64,3712]{1,0:T(8,128)(2,1)S(1)} %collective-permute-done.15.refs_8_.refs_0_.refs_3_), channel_id=1, source_target_pairs={{0,4},{2,6},{4,0},{6,2},{8,12},{10,14},{12,8},{14,10},{16,20},{18,... | collective-permute-start | bytes 1425416 | tf_op jit(solution)/shard_map/ppermute | solution.py:208
  75.0 9.2 %collective-permute-start.19 = (bf16[256,512]{1,0:T(8,128)(2,1)S(1)}, bf16[256,512]{1,0:T(8,128)(2,1)S(1)}, u32[]{:S(2)}, u32[]{:S(2)}) collective-permute-start(bf16[256,512]{1,0:T(8,128)(2,1)S(1)} %shard_map.129.refs_6_.refs_0_), channel_id=1, source_target_pairs={{0,1},{1,0},{2,3},{3,2},{4,5},{5,4},{6,7},{7,6},{8,9},{9,8},{10,11... | collective-permute-start | bytes 786440 | tf_op jit(solution)/shard_map/ppermute | solution.py:204
  79.2 15.4 %collective-permute-start.18 = (bf16[2,256,512]{2,1,0:T(8,128)(2,1)S(1)}, bf16[2,256,512]{2,1,0:T(8,128)(2,1)S(1)}, u32[]{:S(2)}, u32[]{:S(2)}) collective-permute-start(bf16[2,256,512]{2,1,0:T(8,128)(2,1)S(1)} %shard_map.130.refs_7_), channel_id=1, source_target_pairs={{0,1},{1,0},{2,3},{3,2},{4,5},{5,4},{6,7},{7,6},{8,9},{9,8},{10,11... | collective-permute-start | bytes 1572872 | tf_op jit(solution)/shard_map/ppermute | solution.py:204
  90.7 10.4 %collective-permute-start.23 = (bf16[64,3712]{1,0:T(8,128)(2,1)S(1)}, bf16[64,3712]{1,0:T(8,128)(2,1)S(1)}, u32[]{:S(2)}, u32[]{:S(2)}) collective-permute-start(bf16[64,3712]{1,0:T(8,128)(2,1)S(1)} %collective-permute-done.15.refs_8_.refs_0_.refs_3_), channel_id=1, source_target_pairs={{0,2},{2,0},{4,6},{6,4},{8,10},{10,8},{12,14},{14,12},{16,18},{18,... | collective-permute-start | bytes 1425416 | tf_op jit(solution)/shard_map/ppermute | solution.py:208
  97.6 13.3 %collective-permute-start.25 = (bf16[64,3584]{1,0:T(8,128)(2,1)S(1)}, bf16[64,3584]{1,0:T(8,128)(2,1)S(1)}, u32[]{:S(2)}, u32[]{:S(2)}) collective-permute-start(bf16[64,3584]{1,0:T(8,128)(2,1)S(1)} %get-tuple-element.61), channel_id=1, source_target_pairs={{0,2},{2,0},{4,6},{6,4},{8,10},{10,8},{12,14},{14,12},{16,18},{18,... | collective-permute-start | bytes 1376264 | tf_op jit(solution)/shard_map/ppermute | solution.py:208
  98.1 12.8 %collective-permute-start.26 = (bf16[64,3584]{1,0:T(8,128)(2,1)S(1)}, bf16[64,3584]{1,0:T(8,128)(2,1)S(1)}, u32[]{:S(2)}, u32[]{:S(2)}) collective-permute-start(bf16[64,3584]{1,0:T(8,128)(2,1)S(1)} %add_convert_fusion.7.refs_7_), channel_id=1, source_target_pairs={{0,4},{2,6},{4,0},{6,2},{8,12},{10,14},{12,8},{14,10},{16,20},{18,... | collective-permute-start | bytes 1376264 | tf_op jit(solution)/shard_map/ppermute | solution.py:208
  101.0 32.6 %collective-permute-start.11 = (bf16[64,3584]{1,0:T(8,128)(2,1)S(1)}, bf16[64,3584]{1,0:T(8,128)(2,1)S(1)}, u32[]{:S(2)}, u32[]{:S(2)}) collective-permute-start(bf16[64,3584]{1,0:T(8,128)(2,1)S(1)} %get-tuple-element.49), channel_id=1, source_target_pairs={{0,2},{2,0},{4,6},{6,4},{8,10},{10,8},{12,14},{14,12},{16,18},{18,... | collective-permute-start | bytes 1376264 | tf_op jit(solution)/shard_map/ppermute | solution.py:208
  103.8 15.0 %collective-permute-start.28 = (bf16[2,256,512]{2,1,0:T(8,128)(2,1)S(1)}, bf16[2,256,512]{2,1,0:T(8,128)(2,1)S(1)}, u32[]{:S(2)}, u32[]{:S(2)}) collective-permute-start(bf16[2,256,512]{2,1,0:T(8,128)(2,1)S(1)} %shard_map.133.refs_7_), channel_id=1, source_target_pairs={{0,1},{1,0},{2,3},{3,2},{4,5},{5,4},{6,7},{7,6},{8,9},{9,8},{10,11... | collective-permute-start | bytes 1572872 | tf_op jit(solution)/shard_map/ppermute | solution.py:204
  110.8 10.8 %collective-permute-start.30 = (bf16[64,3584]{1,0:T(8,128)(2,1)S(1)}, bf16[64,3584]{1,0:T(8,128)(2,1)S(1)}, u32[]{:S(2)}, u32[]{:S(2)}) collective-permute-start(bf16[64,3584]{1,0:T(8,128)(2,1)S(1)} %get-tuple-element.59.refs_7_), channel_id=1, source_target_pairs={{0,2},{2,0},{4,6},{6,4},{8,10},{10,8},{12,14},{14,12},{16,18},{18,... | collective-permute-start | bytes 1376264 | tf_op jit(solution)/shard_map/ppermute | solution.py:208
  111.1 23.7 %collective-permute-start.31 = (bf16[64,3584]{1,0:T(8,128)(2,1)S(1)}, bf16[64,3584]{1,0:T(8,128)(2,1)S(1)}, u32[]{:S(2)}, u32[]{:S(2)}) collective-permute-start(bf16[64,3584]{1,0:T(8,128)(2,1)S(1)} %add_convert_fusion.6.refs_8_), channel_id=1, source_target_pairs={{0,16},{2,18},{4,20},{6,22},{8,24},{10,26},{12,28},{14,30},{16,0},... | collective-permute-start | bytes 1376264 | tf_op jit(solution)/shard_map/ppermute | solution.py:208
  112.0 21.8 %collective-permute-start.27 = (bf16[64,3584]{1,0:T(8,128)(2,1)S(1)}, bf16[64,3584]{1,0:T(8,128)(2,1)S(1)}, u32[]{:S(2)}, u32[]{:S(2)}) collective-permute-start(bf16[64,3584]{1,0:T(8,128)(2,1)S(1)} %add_convert_fusion.5.refs_9_), channel_id=1, source_target_pairs={{0,4},{2,6},{4,0},{6,2},{8,12},{10,14},{12,8},{14,10},{16,20},{18,... | collective-permute-start | bytes 1376264 | tf_op jit(solution)/shard_map/ppermute | solution.py:208
  118.8 18.4 %collective-permute-start.32 = (bf16[64,3584]{1,0:T(8,128)(2,1)S(1)}, bf16[64,3584]{1,0:T(8,128)(2,1)S(1)}, u32[]{:S(2)}, u32[]{:S(2)}) collective-permute-start(bf16[64,3584]{1,0:T(8,128)(2,1)S(1)} %get-tuple-element.71), channel_id=1, source_target_pairs={{0,2},{2,0},{4,6},{6,4},{8,10},{10,8},{12,14},{14,12},{16,18},{18,... | collective-permute-start | bytes 1376264 | tf_op jit(solution)/shard_map/ppermute | solution.py:208
  121.6 8.8 %collective-permute-start.29 = (bf16[256,512]{1,0:T(8,128)(2,1)S(1)}, bf16[256,512]{1,0:T(8,128)(2,1)S(1)}, u32[]{:S(2)}, u32[]{:S(2)}) collective-permute-start(bf16[256,512]{1,0:T(8,128)(2,1)S(1)} %shard_map.135.refs_0_.refs_7_), channel_id=1, source_target_pairs={{0,1},{1,0},{2,3},{3,2},{4,5},{5,4},{6,7},{7,6},{8,9},{9,8},{10,11... | collective-permute-start | bytes 786440 | tf_op jit(solution)/shard_map/ppermute | solution.py:204
  130.3 13.4 %collective-permute-start.33 = (bf16[64,3584]{1,0:T(8,128)(2,1)S(1)}, bf16[64,3584]{1,0:T(8,128)(2,1)S(1)}, u32[]{:S(2)}, u32[]{:S(2)}) collective-permute-start(bf16[64,3584]{1,0:T(8,128)(2,1)S(1)} %add_convert_fusion.4.refs_8_), channel_id=1, source_target_pairs={{0,4},{2,6},{4,0},{6,2},{8,12},{10,14},{12,8},{14,10},{16,20},{18,... | collective-permute-start | bytes 1376264 | tf_op jit(solution)/shard_map/ppermute | solution.py:208
  133.8 10.8 %collective-permute-start.36 = (bf16[64,3584]{1,0:T(8,128)(2,1)S(1)}, bf16[64,3584]{1,0:T(8,128)(2,1)S(1)}, u32[]{:S(2)}, u32[]{:S(2)}) collective-permute-start(bf16[64,3584]{1,0:T(8,128)(2,1)S(1)} %get-tuple-element.77), channel_id=1, source_target_pairs={{0,2},{2,0},{4,6},{6,4},{8,10},{10,8},{12,14},{14,12},{16,18},{18,... | collective-permute-start | bytes 1376264 | tf_op jit(solution)/shard_map/ppermute | solution.py:208
  135.6 16.7 %collective-permute-start.37 = (bf16[64,3584]{1,0:T(8,128)(2,1)S(1)}, bf16[64,3584]{1,0:T(8,128)(2,1)S(1)}, u32[]{:S(2)}, u32[]{:S(2)}) collective-permute-start(bf16[64,3584]{1,0:T(8,128)(2,1)S(1)} %add_convert_fusion.3), channel_id=1, source_target_pairs={{0,4},{2,6},{4,0},{6,2},{8,12},{10,14},{12,8},{14,10},{16,20},{18,... | collective-permute-start | bytes 1376264 | tf_op jit(solution)/shard_map/ppermute | solution.py:208
  143.9 13.5 %collective-permute-start.35 = (bf16[64,3584]{1,0:T(8,128)(2,1)S(1)}, bf16[64,3584]{1,0:T(8,128)(2,1)S(1)}, u32[]{:S(2)}, u32[]{:S(2)}) collective-permute-start(bf16[64,3584]{1,0:T(8,128)(2,1)S(1)} %add_convert_fusion.2), channel_id=1, source_target_pairs={{0,24},{2,26},{4,28},{6,30},{8,16},{10,18},{12,20},{14,22},{16,8},... | collective-permute-start | bytes 1376264 | tf_op jit(solution)/shard_map/ppermute | solution.py:208
  152.5 13.2 %collective-permute-start.38 = (bf16[64,3584]{1,0:T(8,128)(2,1)S(1)}, bf16[64,3584]{1,0:T(8,128)(2,1)S(1)}, u32[]{:S(2)}, u32[]{:S(2)}) collective-permute-start(bf16[64,3584]{1,0:T(8,128)(2,1)S(1)} %add_convert_fusion.1), channel_id=1, source_target_pairs={{0,8},{2,10},{4,12},{6,14},{8,0},{10,2},{12,4},{14,6},{16,24},{18,... | collective-permute-start | bytes 1376264 | tf_op jit(solution)/shard_map/ppermute | solution.py:208
  (7 other events, 30.0 us)

commit v2 on v0

--- a/solution.py
+++ b/solution.py
@@ -240,11 +240,8 @@
     groups = 4
     per_group = z_count // groups
     members = [[group * per_group + i for i in range(per_group)] for group in (0, 2, 3, 1)]
-    early = {0: both}
-    for group in (members[0], members[1], members[3], members[2]):
-        for r in group:
-            early[r] = early.get(r) if r == 0 else flipped(both, ep, 4 * r)
-    along_z = [[early[r] for r in group] for group in members]
+    along_z = [[both if r == 0 else flipped(both, ep, 4 * r) for r in members[g]] for g in (0, 1, 3)]
+    along_z.insert(2, [flipped(value, ep, 4 * per_group) for value in along_z[1]])
     gate_weight, up_weight = load([gate_weight, up_weight], [both, scalars])
     (down_weight,) = load([down_weight], [gate_weight])
     state = [dict() for _ in range(groups)]
@@ -269,6 +266,9 @@
 
     def hold_x(g):
         last.extend(state[g]["across"])
+
+    def hold_blocks(g):
+        last.extend(state[g]["blocks"])
 
     def hold_core(g):
         last.append(state[g]["core_far"])
@@ -331,10 +331,10 @@
         for stage, g in turns:
             stage(g)
 
-    run((ask_x, 0), (ask_core, 0), (hold_z, 1), (send_sums, 0), (ask_x, 1), (hold_x, 1), (send_hidden, 0), (ask_core, 1))
-    run((hold_z, 2), (send_sums, 1), (ask_x, 2), (send_core, 0), (hold_x, 2), (send_hidden, 1), (hold_core, 0), (hold_z, 3))
-    run((ask_core, 2), (ask_x, 3), (send_sums, 2), (hold_x, 3), (send_core, 1), (send_hidden, 2), (send_x, 1))
-    run((ask_core, 3), (send_sums, 3), (send_core, 2), (send_z, 1), (send_x, 0), (send_hidden, 3), (send_x, 2))
+    run((ask_x, 0), (ask_core, 0), (hold_z, 3), (hold_z, 1), (send_sums, 0), (ask_x, 1), (hold_x, 1), (send_hidden, 0), (hold_z, 2), (ask_core, 1), (ask_x, 2))
+    run((send_sums, 1), (send_core, 0), (hold_x, 2), (send_hidden, 1), (hold_core, 0), (ask_core, 2), (ask_x, 3))
+    run((send_sums, 2), (hold_x, 3), (send_core, 1), (send_hidden, 2), (send_x, 1), (ask_core, 3), (send_sums, 3))
+    run((send_core, 2), (send_z, 1), (send_x, 0), (send_hidden, 3), (send_x, 2))
     run((send_core, 3), (send_z, 0), (finish, 0), (finish, 1), (send_x, 3), (send_z, 2), (send_z, 3), (finish, 2), (finish, 3))
     total = totals[-1]
     return total[:row_count].astype(BF16), total[row_count:].astype(BF16)

time: 163 us -> 163 us (level)
  starting transfers between devices: 51.1 us -> 36.3 us
  waiting for transfers between devices: 62.6 us -> 77.3 us
    ppermute x30, starting transfers between devices: 40.2 us -> 25.9 us  [flipped(): return lax.ppermute(value, 'ep', [(i, i ^ bits) for i in range(size)])]
    ppermute x30, waiting for transfers between devices: 42.3 us -> 49.9 us  [flipped(): return lax.ppermute(value, 'ep', [(i, i ^ bits) for i in range(size)])]
    ppermute x8, waiting for transfers between devices: 20.2 us -> 27.4 us  [shifted(): lax.ppermute(value, axis, [(i, (i + step) % size) for i in range(size)])]
  transfers between devices with their start and end apart: 38 -> 38, of which waited for: 16 -> 19; matrix products, arithmetic and copies ran while one was open for 3% -> 3% of each run, Pallas kernels for 24% -> 24%
where the time goes in v2:
time: 163 us
  waiting for transfers between devices  77.3 us (47%)
  Pallas kernels  42.6 us (26%)
  starting transfers between devices  36.3 us (22%)
  other arithmetic  3.82 us (2%)
    ppermute x30, waiting for transfers between devices, flipped(): return lax.ppermute(value, 'ep', [(i, i ^ bits) for i in range(size)])  49.9 us
    ppermute x8, waiting for transfers between devices, shifted(): lax.ppermute(value, axis, [(i, (i + step) % size) for i in range(size)])  27.4 us
    ppermute x30, starting transfers between devices, flipped(): return lax.ppermute(value, 'ep', [(i, i ^ bits) for i in range(size)])  25.9 us
    pallas_call x8, Pallas kernels, sums(): pl.pallas_call(functools.partial(sums_kernel, len(blocks), len(arrived),...  21.9 us
    pallas_call x4, Pallas kernels, down_rows(): pl.pallas_call(functools.partial(down_kernel, parts, len(blocks), len(aft...  11.1 us
    ppermute x8, starting transfers between devices, shifted(): lax.ppermute(value, axis, [(i, (i + step) % size) for i in range(size)])  10.4 us
    pallas_call x2, Pallas kernels, load(): pl.pallas_call(lambda *refs: load_kernel(count, *refs[:count], *refs[coun...  8.29 us
  transfers between devices with their start and end apart: 38, of which 19 were waited for; matrix products, arithmetic and copies ran while one was open for 3% of the time, Pallas kernels for 24%

profile of v2, /device:TPU:0, one launch (start us, length us, event | category | flops | bytes accessed | tf_op | source)
XLA Modules:
  0.0 163.2 jit_solution(3732926167849784597)
XLA Ops:
  1.9 3.0 %collective-permute-start = (bf16[64,3712]{1,0:T(8,128)(2,1)S(1)}, bf16[64,3712]{1,0:T(8,128)(2,1)S(1)}, u32[]{:S(2)}, u32[]{:S(2)}) collective-permute-start(bf16[64,3712]{1,0:T(8,128)(2,1)S(1)} %shard_map.122.refs_2_.refs_0_.refs_3_), channel_id=1, source_target_pairs={{0,4},{2,6},{4,0},{6,2},{8,12},{10,14},{12,8},{14,10},{16,20},{18,... | collective-permute-start | bytes 1425416 | tf_op jit(solution)/shard_map/ppermute | solution.py:205
  4.9 2.6 %collective-permute-start.4 = (bf16[64,3712]{1,0:T(8,128)(2,1)S(1)}, bf16[64,3712]{1,0:T(8,128)(2,1)S(1)}, u32[]{:S(2)}, u32[]{:S(2)}) collective-permute-start(bf16[64,3712]{1,0:T(8,128)(2,1)S(1)} %shard_map.122.refs_2_.refs_0_.refs_3_), channel_id=1, source_target_pairs={{0,16},{2,18},{4,20},{6,22},{8,24},{10,26},{12,28},{14,30},{16,0},... | collective-permute-start | bytes 1425416 | tf_op jit(solution)/shard_map/ppermute | solution.py:205
  13.1 5.2 %shard_map.123 = (bf16[1,3584,1024]{2,1,0:T(8,128)(2,1)S(1)}, bf16[1,3584,1024]{2,1,0:T(8,128)(2,1)S(1)}) custom-call(bf16[1,3584,1024]{2,1,0:T(8,128)(2,1)} %refs_0_.2, bf16[1,3584,1024]{2,1,0:T(8,128)(2,1)} %refs_1_.1, bf16[64,3712]{1,0:T(8,128)(2,1)S(1)} %shard_map.122.refs_2_.refs_0_.refs_3_, s32[5]{0:T(128)S(1)} %stack.23.refs_3_.scalar_ref), custom_call_target="tpu_custom_call" | custom-call | flops 1 | bytes 1 | tf_op jit(solution)/shard_map/pallas_call | solution.py:53
  18.3 3.1 %shard_map.124.refs_6_.refs_2_ = bf16[1,1024,3584]{2,1,0:T(8,128)(2,1)S(1)} custom-call(bf16[1,1024,3584]{2,1,0:T(8,128)(2,1)} %refs_0_.3, bf16[1,3584,1024]{2,1,0:T(8,128)(2,1)S(1)} %get-tuple-element.39.refs_1_.refs_4_), custom_call_target="tpu_custom_call" | custom-call | flops 1 | bytes 1 | tf_op jit(solution)/shard_map/pallas_call | solution.py:53
  22.0 6.5 %collective-permute-done.4.refs_8_.refs_0_.refs_3_ = bf16[64,3712]{1,0:T(8,128)(2,1)S(1)} collective-permute-done((bf16[64,3712]{1,0:T(8,128)(2,1)S(1)}, bf16[64,3712]{1,0:T(8,128)(2,1)S(1)}, u32[]{:S(2)}, u32[]{:S(2)}) %collective-permute-start.4) | collective-permute-done | bytes 475168 | tf_op jit(solution)/shard_map/ppermute | solution.py:205
  28.7 2.7 %shard_map.125.refs_7_ = bf16[2,256,512]{2,1,0:T(8,128)(2,1)S(1)} custom-call(s32[5]{0:T(128)S(1)} %stack.23.refs_3_.scalar_ref, bf16[64,3712]{1,0:T(8,128)(2,1)S(1)} %shard_map.122.refs_2_.refs_0_.refs_3_, bf16[64,3712]{1,0:T(8,128)(2,1)S(1)} %collective-permute-done.refs_1_.refs_4_, bf16[64,3712]{1,0:T(8,128)(2,1)S(1)} %collective-permute-done.1.refs_2_.refs_5_, ...), custom_call_target="tpu_custom_call" | custom-call | flops 1 | bytes 1 | tf_op jit(solution)/shard_map/pallas_call | solution.py:97
  34.9 9.2 %collective-permute-done.6.refs_8_.refs_1_.refs_4_ = bf16[64,3712]{1,0:T(8,128)(2,1)S(1)} collective-permute-done((bf16[64,3712]{1,0:T(8,128)(2,1)S(1)}, bf16[64,3712]{1,0:T(8,128)(2,1)S(1)}, u32[]{:S(2)}, u32[]{:S(2)}) %collective-permute-start.6) | collective-permute-done | bytes 475168 | tf_op jit(solution)/shard_map/ppermute | solution.py:205
  44.2 2.8 %shard_map.126.refs_6_.refs_0_ = bf16[256,512]{1,0:T(8,128)(2,1)S(1)} custom-call(s32[5]{0:T(128)S(1)} %stack.23.refs_3_.scalar_ref, bf16[64,3712]{1,0:T(8,128)(2,1)S(1)} %shard_map.122.refs_2_.refs_0_.refs_3_, bf16[64,3712]{1,0:T(8,128)(2,1)S(1)} %collective-permute-done.refs_1_.refs_4_, bf16[64,3712]{1,0:T(8,128)(2,1)S(1)} %collective-permute-done.1.refs_2_.refs_5_, ...), custom_call_target="tpu_custom_call" | custom-call | flops 1 | bytes 1 | tf_op jit(solution)/shard_map/pallas_call | solution.py:97
  48.9 2.7 %shard_map.127.refs_7_ = bf16[2,256,512]{2,1,0:T(8,128)(2,1)S(1)} custom-call(s32[5]{0:T(128)S(1)} %stack.23.refs_3_.scalar_ref, bf16[64,3712]{1,0:T(8,128)(2,1)S(1)} %collective-permute-done.4.refs_8_.refs_0_.refs_3_, bf16[64,3712]{1,0:T(8,128)(2,1)S(1)} %collective-permute-done.6.refs_8_.refs_1_.refs_4_, ...), custom_call_target="tpu_custom_call" | custom-call | flops 1 | bytes 1 | tf_op jit(solution)/shard_map/pallas_call | solution.py:97
  53.5 2.8 %collective-permute-done.7.refs_1_ = bf16[256,512]{1,0:T(8,128)(2,1)S(1)} collective-permute-done((bf16[256,512]{1,0:T(8,128)(2,1)S(1)}, bf16[256,512]{1,0:T(8,128)(2,1)S(1)}, u32[]{:S(2)}, u32[]{:S(2)}) %collective-permute-start.7) | collective-permute-done | bytes 262176 | tf_op jit(solution)/shard_map/ppermute | solution.py:201
  56.2 2.7 %shard_map.128 = (f32[64,3584]{1,0:T(8,128)S(1)}, f32[64,3584]{1,0:T(8,128)S(1)}, bf16[64,3584]{1,0:T(8,128)(2,1)S(1)}, bf16[64,3584]{1,0:T(8,128)(2,1)S(1)}) custom-call(s32[5]{0:T(128)S(1)} %stack.23.refs_3_.scalar_ref, bf16[256,512]{1,0:T(8,128)(2,1)S(1)} %shard_map.126.refs_6_.refs_0_, bf16[256,512]{1,0:T(8,128)(2,1)S(1)} %collective-permute-done.7.refs_1_, ...), custom_call_target="tpu_custom_call" | custom-call | flops 1 | bytes 1 | tf_op jit(solution)/shard_map/pallas_call | solution.py:144
  59.5 6.0 %collective-permute-done.13.refs_8_.refs_1_.refs_4_ = bf16[64,3712]{1,0:T(8,128)(2,1)S(1)} collective-permute-done((bf16[64,3712]{1,0:T(8,128)(2,1)S(1)}, bf16[64,3712]{1,0:T(8,128)(2,1)S(1)}, u32[]{:S(2)}, u32[]{:S(2)}) %collective-permute-start.13) | collective-permute-done | bytes 475168 | tf_op jit(solution)/shard_map/ppermute | solution.py:205
  67.0 2.8 %shard_map.129.refs_6_.refs_0_ = bf16[256,512]{1,0:T(8,128)(2,1)S(1)} custom-call(s32[5]{0:T(128)S(1)} %stack.23.refs_3_.scalar_ref, bf16[64,3712]{1,0:T(8,128)(2,1)S(1)} %collective-permute-done.4.refs_8_.refs_0_.refs_3_, bf16[64,3712]{1,0:T(8,128)(2,1)S(1)} %collective-permute-done.6.refs_8_.refs_1_.refs_4_, ...), custom_call_target="tpu_custom_call" | custom-call | flops 1 | bytes 1 | tf_op jit(solution)/shard_map/pallas_call | solution.py:97
  71.8 2.7 %shard_map.130.refs_7_ = bf16[2,256,512]{2,1,0:T(8,128)(2,1)S(1)} custom-call(s32[5]{0:T(128)S(1)} %stack.23.refs_3_.scalar_ref, bf16[64,3712]{1,0:T(8,128)(2,1)S(1)} %collective-permute-done.8.refs_7_.refs_0_.refs_3_, bf16[64,3712]{1,0:T(8,128)(2,1)S(1)} %collective-permute-done.13.refs_8_.refs_1_.refs_4_, ...), custom_call_target="tpu_custom_call" | custom-call | flops 1 | bytes 1 | tf_op jit(solution)/shard_map/pallas_call | solution.py:97
  75.8 3.8 %collective-permute-done.18.refs_1_ = bf16[256,512]{1,0:T(8,128)(2,1)S(1)} collective-permute-done((bf16[256,512]{1,0:T(8,128)(2,1)S(1)}, bf16[256,512]{1,0:T(8,128)(2,1)S(1)}, u32[]{:S(2)}, u32[]{:S(2)}) %collective-permute-start.18) | collective-permute-done | bytes 262176 | tf_op jit(solution)/shard_map/ppermute | solution.py:201
  79.6 3.5 %collective-permute-done.19.refs_8_.refs_1_.refs_4_ = bf16[64,3712]{1,0:T(8,128)(2,1)S(1)} collective-permute-done((bf16[64,3712]{1,0:T(8,128)(2,1)S(1)}, bf16[64,3712]{1,0:T(8,128)(2,1)S(1)}, u32[]{:S(2)}, u32[]{:S(2)}) %collective-permute-start.19) | collective-permute-done | bytes 475168 | tf_op jit(solution)/shard_map/ppermute | solution.py:205
  83.1 2.9 %shard_map.131 = (f32[64,3584]{1,0:T(8,128)S(1)}, f32[64,3584]{1,0:T(8,128)S(1)}, bf16[64,3584]{1,0:T(8,128)(2,1)S(1)}, bf16[64,3584]{1,0:T(8,128)(2,1)S(1)}) custom-call(s32[5]{0:T(128)S(1)} %stack.23.refs_3_.scalar_ref, bf16[256,512]{1,0:T(8,128)(2,1)S(1)} %shard_map.129.refs_6_.refs_0_, bf16[256,512]{1,0:T(8,128)(2,1)S(1)} %collective-permute-done.18.refs_1_, ...), custom_call_target="tpu_custom_call" | custom-call | flops 1 | bytes 1 | tf_op jit(solution)/shard_map/pallas_call | solution.py:144
  86.6 3.4 %collective-permute-done.17.refs_6_ = bf16[2,256,512]{2,1,0:T(8,128)(2,1)S(1)} collective-permute-done((bf16[2,256,512]{2,1,0:T(8,128)(2,1)S(1)}, bf16[2,256,512]{2,1,0:T(8,128)(2,1)S(1)}, u32[]{:S(2)}, u32[]{:S(2)}) %collective-permute-start.17) | collective-permute-done | bytes 524320 | tf_op jit(solution)/shard_map/ppermute | solution.py:201
  90.1 2.8 %shard_map.132.refs_6_.refs_0_ = bf16[256,512]{1,0:T(8,128)(2,1)S(1)} custom-call(s32[5]{0:T(128)S(1)} %stack.23.refs_3_.scalar_ref, bf16[64,3712]{1,0:T(8,128)(2,1)S(1)} %collective-permute-done.8.refs_7_.refs_0_.refs_3_, bf16[64,3712]{1,0:T(8,128)(2,1)S(1)} %collective-permute-done.13.refs_8_.refs_1_.refs_4_, ...), custom_call_target="tpu_custom_call" | custom-call | flops 1 | bytes 1 | tf_op jit(solution)/shard_map/pallas_call | solution.py:97
  96.3 2.7 %shard_map.133.refs_7_ = bf16[2,256,512]{2,1,0:T(8,128)(2,1)S(1)} custom-call(s32[5]{0:T(128)S(1)} %stack.23.refs_3_.scalar_ref, bf16[64,3712]{1,0:T(8,128)(2,1)S(1)} %collective-permute-done.3.refs_7_.refs_0_.refs_3_, bf16[64,3712]{1,0:T(8,128)(2,1)S(1)} %collective-permute-done.19.refs_8_.refs_1_.refs_4_, ...), custom_call_target="tpu_custom_call" | custom-call | flops 1 | bytes 1 | tf_op jit(solution)/shard_map/pallas_call | solution.py:97
  99.9 4.0 %collective-permute-done.20.refs_1_ = bf16[256,512]{1,0:T(8,128)(2,1)S(1)} collective-permute-done((bf16[256,512]{1,0:T(8,128)(2,1)S(1)}, bf16[256,512]{1,0:T(8,128)(2,1)S(1)}, u32[]{:S(2)}, u32[]{:S(2)}) %collective-permute-start.20) | collective-permute-done | bytes 262176 | tf_op jit(solution)/shard_map/ppermute | solution.py:201
  103.8 2.7 %shard_map.134 = (f32[64,3584]{1,0:T(8,128)S(1)}, f32[64,3584]{1,0:T(8,128)S(1)}, bf16[64,3584]{1,0:T(8,128)(2,1)S(1)}, bf16[64,3584]{1,0:T(8,128)(2,1)S(1)}) custom-call(s32[5]{0:T(128)S(1)} %stack.23.refs_3_.scalar_ref, bf16[256,512]{1,0:T(8,128)(2,1)S(1)} %shard_map.132.refs_6_.refs_0_, bf16[256,512]{1,0:T(8,128)(2,1)S(1)} %collective-permute-done.20.refs_1_, ...), custom_call_target="tpu_custom_call" | custom-call | flops 1 | bytes 1 | tf_op jit(solution)/shard_map/pallas_call | solution.py:144
  109.6 4.7 %collective-permute-done.27.refs_6_ = bf16[2,256,512]{2,1,0:T(8,128)(2,1)S(1)} collective-permute-done((bf16[2,256,512]{2,1,0:T(8,128)(2,1)S(1)}, bf16[2,256,512]{2,1,0:T(8,128)(2,1)S(1)}, u32[]{:S(2)}, u32[]{:S(2)}) %collective-permute-start.27) | collective-permute-done | bytes 524320 | tf_op jit(solution)/shard_map/ppermute | solution.py:201
  114.3 2.8 %shard_map.135.refs_0_.refs_7_ = bf16[256,512]{1,0:T(8,128)(2,1)S(1)} custom-call(s32[5]{0:T(128)S(1)} %stack.23.refs_3_.scalar_ref, bf16[64,3712]{1,0:T(8,128)(2,1)S(1)} %collective-permute-done.3.refs_7_.refs_0_.refs_3_, bf16[64,3712]{1,0:T(8,128)(2,1)S(1)} %collective-permute-done.19.refs_8_.refs_1_.refs_4_, ...), custom_call_target="tpu_custom_call" | custom-call | flops 1 | bytes 1 | tf_op jit(solution)/shard_map/pallas_call | solution.py:97
  118.5 7.4 %collective-permute-done.28.refs_1_ = bf16[256,512]{1,0:T(8,128)(2,1)S(1)} collective-permute-done((bf16[256,512]{1,0:T(8,128)(2,1)S(1)}, bf16[256,512]{1,0:T(8,128)(2,1)S(1)}, u32[]{:S(2)}, u32[]{:S(2)}) %collective-permute-start.28) | collective-permute-done | bytes 262176 | tf_op jit(solution)/shard_map/ppermute | solution.py:201
  126.4 2.7 %shard_map.136 = (f32[64,3584]{1,0:T(8,128)S(1)}, f32[64,3584]{1,0:T(8,128)S(1)}, bf16[64,3584]{1,0:T(8,128)(2,1)S(1)}, bf16[64,3584]{1,0:T(8,128)(2,1)S(1)}) custom-call(s32[5]{0:T(128)S(1)} %stack.23.refs_3_.scalar_ref, bf16[256,512]{1,0:T(8,128)(2,1)S(1)} %shard_map.135.refs_0_.refs_7_, bf16[256,512]{1,0:T(8,128)(2,1)S(1)} %collective-permute-done.28.refs_1_, ...), custom_call_target="tpu_custom_call" | custom-call | flops 1 | bytes 1 | tf_op jit(solution)/shard_map/pallas_call | solution.py:144
  132.7 6.6 %collective-permute-done.32 = bf16[64,3584]{1,0:T(8,128)(2,1)S(1)} collective-permute-done((bf16[64,3584]{1,0:T(8,128)(2,1)S(1)}, bf16[64,3584]{1,0:T(8,128)(2,1)S(1)}, u32[]{:S(2)}, u32[]{:S(2)}) %collective-permute-start.32) | collective-permute-done | bytes 458784 | tf_op jit(solution)/shard_map/ppermute | solution.py:205
  139.5 4.6 %collective-permute-start.34 = (bf16[64,3584]{1,0:T(8,128)(2,1)S(1)}, bf16[64,3584]{1,0:T(8,128)(2,1)S(1)}, u32[]{:S(2)}, u32[]{:S(2)}) collective-permute-start(bf16[64,3584]{1,0:T(8,128)(2,1)S(1)} %add_convert_fusion.2), channel_id=1, source_target_pairs={{0,24},{2,26},{4,28},{6,30},{8,16},{10,18},{12,20},{14,22},{16,8},... | collective-permute-start | bytes 1376264 | tf_op jit(solution)/shard_map/ppermute | solution.py:205
  144.1 3.8 %collective-permute-done.36 = bf16[64,3584]{1,0:T(8,128)(2,1)S(1)} collective-permute-done((bf16[64,3584]{1,0:T(8,128)(2,1)S(1)}, bf16[64,3584]{1,0:T(8,128)(2,1)S(1)}, u32[]{:S(2)}, u32[]{:S(2)}) %collective-permute-start.36) | collective-permute-done | bytes 458784 | tf_op jit(solution)/shard_map/ppermute | solution.py:205
  148.0 1.8 %collective-permute-start.37 = (bf16[64,3584]{1,0:T(8,128)(2,1)S(1)}, bf16[64,3584]{1,0:T(8,128)(2,1)S(1)}, u32[]{:S(2)}, u32[]{:S(2)}) collective-permute-start(bf16[64,3584]{1,0:T(8,128)(2,1)S(1)} %add_convert_fusion.1), channel_id=1, source_target_pairs={{0,8},{2,10},{4,12},{6,14},{8,0},{10,2},{12,4},{14,6},{16,24},{18,... | collective-permute-start | bytes 1376264 | tf_op jit(solution)/shard_map/ppermute | solution.py:205
  149.8 4.6 %collective-permute-done.34 = bf16[64,3584]{1,0:T(8,128)(2,1)S(1)} collective-permute-done((bf16[64,3584]{1,0:T(8,128)(2,1)S(1)}, bf16[64,3584]{1,0:T(8,128)(2,1)S(1)}, u32[]{:S(2)}, u32[]{:S(2)}) %collective-permute-start.34) | collective-permute-done | bytes 458784 | tf_op jit(solution)/shard_map/ppermute | solution.py:205
  154.4 7.9 %collective-permute-done.37 = bf16[64,3584]{1,0:T(8,128)(2,1)S(1)} collective-permute-done((bf16[64,3584]{1,0:T(8,128)(2,1)S(1)}, bf16[64,3584]{1,0:T(8,128)(2,1)S(1)}, u32[]{:S(2)}, u32[]{:S(2)}) %collective-permute-start.37) | collective-permute-done | bytes 458784 | tf_op jit(solution)/shard_map/ppermute | solution.py:205
  (73 shorter events, 34.3 us)
Async XLA Ops:
  1.9 19.5 %collective-permute-start = (bf16[64,3712]{1,0:T(8,128)(2,1)S(1)}, bf16[64,3712]{1,0:T(8,128)(2,1)S(1)}, u32[]{:S(2)}, u32[]{:S(2)}) collective-permute-start(bf16[64,3712]{1,0:T(8,128)(2,1)S(1)} %shard_map.122.refs_2_.refs_0_.refs_3_), channel_id=1, source_target_pairs={{0,4},{2,6},{4,0},{6,2},{8,12},{10,14},{12,8},{14,10},{16,20},{18,... | collective-permute-start | bytes 1425416 | tf_op jit(solution)/shard_map/ppermute | solution.py:205
  4.9 23.5 %collective-permute-start.4 = (bf16[64,3712]{1,0:T(8,128)(2,1)S(1)}, bf16[64,3712]{1,0:T(8,128)(2,1)S(1)}, u32[]{:S(2)}, u32[]{:S(2)}) collective-permute-start(bf16[64,3712]{1,0:T(8,128)(2,1)S(1)} %shard_map.122.refs_2_.refs_0_.refs_3_), channel_id=1, source_target_pairs={{0,16},{2,18},{4,20},{6,22},{8,24},{10,26},{12,28},{14,30},{16,0},... | collective-permute-start | bytes 1425416 | tf_op jit(solution)/shard_map/ppermute | solution.py:205
  7.5 21.1 %collective-permute-start.3 = (bf16[64,3712]{1,0:T(8,128)(2,1)S(1)}, bf16[64,3712]{1,0:T(8,128)(2,1)S(1)}, u32[]{:S(2)}, u32[]{:S(2)}) collective-permute-start(bf16[64,3712]{1,0:T(8,128)(2,1)S(1)} %shard_map.122.refs_2_.refs_0_.refs_3_), channel_id=1, source_target_pairs={{0,8},{2,10},{4,12},{6,14},{8,0},{10,2},{12,4},{14,6},{16,24},{18,... | collective-permute-start | bytes 1425416 | tf_op jit(solution)/shard_map/ppermute | solution.py:205
  9.1 19.5 %collective-permute-start.1 = (bf16[64,3712]{1,0:T(8,128)(2,1)S(1)}, bf16[64,3712]{1,0:T(8,128)(2,1)S(1)}, u32[]{:S(2)}, u32[]{:S(2)}) collective-permute-start(bf16[64,3712]{1,0:T(8,128)(2,1)S(1)} %shard_map.122.refs_2_.refs_0_.refs_3_), channel_id=1, source_target_pairs={{0,2},{2,0},{4,6},{6,4},{8,10},{10,8},{12,14},{14,12},{16,18},{18,... | collective-permute-start | bytes 1425416 | tf_op jit(solution)/shard_map/ppermute | solution.py:205
  31.3 12.8 %collective-permute-start.5 = (bf16[2,256,512]{2,1,0:T(8,128)(2,1)S(1)}, bf16[2,256,512]{2,1,0:T(8,128)(2,1)S(1)}, u32[]{:S(2)}, u32[]{:S(2)}) collective-permute-start(bf16[2,256,512]{2,1,0:T(8,128)(2,1)S(1)} %shard_map.125.refs_7_), channel_id=1, source_target_pairs={{0,1},{1,0},{2,3},{3,2},{4,5},{5,4},{6,7},{7,6},{8,9},{9,8},{10,11... | collective-permute-start | bytes 1572872 | tf_op jit(solution)/shard_map/ppermute | solution.py:201
  33.0 11.2 %collective-permute-start.6 = (bf16[64,3712]{1,0:T(8,128)(2,1)S(1)}, bf16[64,3712]{1,0:T(8,128)(2,1)S(1)}, u32[]{:S(2)}, u32[]{:S(2)}) collective-permute-start(bf16[64,3712]{1,0:T(8,128)(2,1)S(1)} %collective-permute-done.4.refs_8_.refs_0_.refs_3_), channel_id=1, source_target_pairs={{0,4},{2,6},{4,0},{6,2},{8,12},{10,14},{12,8},{14,10},{16,20},{18,... | collective-permute-start | bytes 1425416 | tf_op jit(solution)/shard_map/ppermute | solution.py:205
  33.5 13.4 %collective-permute-start.8 = (bf16[64,3712]{1,0:T(8,128)(2,1)S(1)}, bf16[64,3712]{1,0:T(8,128)(2,1)S(1)}, u32[]{:S(2)}, u32[]{:S(2)}) collective-permute-start(bf16[64,3712]{1,0:T(8,128)(2,1)S(1)} %collective-permute-done.4.refs_8_.refs_0_.refs_3_), channel_id=1, source_target_pairs={{0,8},{2,10},{4,12},{6,14},{8,0},{10,2},{12,4},{14,6},{16,24},{18,... | collective-permute-start | bytes 1425416 | tf_op jit(solution)/shard_map/ppermute | solution.py:205
  34.9 13.5 %collective-permute-start.9 = (bf16[64,3712]{1,0:T(8,128)(2,1)S(1)}, bf16[64,3712]{1,0:T(8,128)(2,1)S(1)}, u32[]{:S(2)}, u32[]{:S(2)}) collective-permute-start(bf16[64,3712]{1,0:T(8,128)(2,1)S(1)} %collective-permute-done.4.refs_8_.refs_0_.refs_3_), channel_id=1, source_target_pairs={{0,2},{2,0},{4,6},{6,4},{8,10},{10,8},{12,14},{14,12},{16,18},{18,... | collective-permute-start | bytes 1425416 | tf_op jit(solution)/shard_map/ppermute | solution.py:205
  47.0 9.2 %collective-permute-start.7 = (bf16[256,512]{1,0:T(8,128)(2,1)S(1)}, bf16[256,512]{1,0:T(8,128)(2,1)S(1)}, u32[]{:S(2)}, u32[]{:S(2)}) collective-permute-start(bf16[256,512]{1,0:T(8,128)(2,1)S(1)} %shard_map.126.refs_6_.refs_0_), channel_id=1, source_target_pairs={{0,1},{1,0},{2,3},{3,2},{4,5},{5,4},{6,7},{7,6},{8,9},{9,8},{10,11... | collective-permute-start | bytes 786440 | tf_op jit(solution)/shard_map/ppermute | solution.py:201
  51.6 15.4 %collective-permute-start.14 = (bf16[2,256,512]{2,1,0:T(8,128)(2,1)S(1)}, bf16[2,256,512]{2,1,0:T(8,128)(2,1)S(1)}, u32[]{:S(2)}, u32[]{:S(2)}) collective-permute-start(bf16[2,256,512]{2,1,0:T(8,128)(2,1)S(1)} %shard_map.127.refs_7_), channel_id=1, source_target_pairs={{0,1},{1,0},{2,3},{3,2},{4,5},{5,4},{6,7},{7,6},{8,9},{9,8},{10,11... | collective-permute-start | bytes 1572872 | tf_op jit(solution)/shard_map/ppermute | solution.py:201
  52.9 12.6 %collective-permute-start.13 = (bf16[64,3712]{1,0:T(8,128)(2,1)S(1)}, bf16[64,3712]{1,0:T(8,128)(2,1)S(1)}, u32[]{:S(2)}, u32[]{:S(2)}) collective-permute-start(bf16[64,3712]{1,0:T(8,128)(2,1)S(1)} %collective-permute-done.8.refs_7_.refs_0_.refs_3_), channel_id=1, source_target_pairs={{0,4},{2,6},{4,0},{6,2},{8,12},{10,14},{12,8},{14,10},{16,20},{18,... | collective-permute-start | bytes 1425416 | tf_op jit(solution)/shard_map/ppermute | solution.py:205
  58.9 10.8 %collective-permute-start.12 = (bf16[64,3584]{1,0:T(8,128)(2,1)S(1)}, bf16[64,3584]{1,0:T(8,128)(2,1)S(1)}, u32[]{:S(2)}, u32[]{:S(2)}) collective-permute-start(bf16[64,3584]{1,0:T(8,128)(2,1)S(1)} %get-tuple-element.47.refs_7_), channel_id=1, source_target_pairs={{0,2},{2,0},{4,6},{6,4},{8,10},{10,8},{12,14},{14,12},{16,18},{18,... | collective-permute-start | bytes 1376264 | tf_op jit(solution)/shard_map/ppermute | solution.py:205
  59.0 12.7 %collective-permute-start.15 = (bf16[64,3712]{1,0:T(8,128)(2,1)S(1)}, bf16[64,3712]{1,0:T(8,128)(2,1)S(1)}, u32[]{:S(2)}, u32[]{:S(2)}) collective-permute-start(bf16[64,3712]{1,0:T(8,128)(2,1)S(1)} %collective-permute-done.8.refs_7_.refs_0_.refs_3_), channel_id=1, source_target_pairs={{0,2},{2,0},{4,6},{6,4},{8,10},{10,8},{12,14},{14,12},{16,18},{18,... | collective-permute-start | bytes 1425416 | tf_op jit(solution)/shard_map/ppermute | solution.py:205
  69.8 13.3 %collective-permute-start.19 = (bf16[64,3712]{1,0:T(8,128)(2,1)S(1)}, bf16[64,3712]{1,0:T(8,128)(2,1)S(1)}, u32[]{:S(2)}, u32[]{:S(2)}) collective-permute-start(bf16[64,3712]{1,0:T(8,128)(2,1)S(1)} %collective-permute-done.3.refs_7_.refs_0_.refs_3_), channel_id=1, source_target_pairs={{0,4},{2,6},{4,0},{6,2},{8,12},{10,14},{12,8},{14,10},{16,20},{18,... | collective-permute-start | bytes 1425416 | tf_op jit(solution)/shard_map/ppermute | solution.py:205
  70.5 9.2 %collective-permute-start.18 = (bf16[256,512]{1,0:T(8,128)(2,1)S(1)}, bf16[256,512]{1,0:T(8,128)(2,1)S(1)}, u32[]{:S(2)}, u32[]{:S(2)}) collective-permute-start(bf16[256,512]{1,0:T(8,128)(2,1)S(1)} %shard_map.129.refs_6_.refs_0_), channel_id=1, source_target_pairs={{0,1},{1,0},{2,3},{3,2},{4,5},{5,4},{6,7},{7,6},{8,9},{9,8},{10,11... | collective-permute-start | bytes 786440 | tf_op jit(solution)/shard_map/ppermute | solution.py:201
  74.5 15.6 %collective-permute-start.17 = (bf16[2,256,512]{2,1,0:T(8,128)(2,1)S(1)}, bf16[2,256,512]{2,1,0:T(8,128)(2,1)S(1)}, u32[]{:S(2)}, u32[]{:S(2)}) collective-permute-start(bf16[2,256,512]{2,1,0:T(8,128)(2,1)S(1)} %shard_map.130.refs_7_), channel_id=1, source_target_pairs={{0,1},{1,0},{2,3},{3,2},{4,5},{5,4},{6,7},{7,6},{8,9},{9,8},{10,11... | collective-permute-start | bytes 1572872 | tf_op jit(solution)/shard_map/ppermute | solution.py:201
  86.2 10.2 %collective-permute-start.22 = (bf16[64,3712]{1,0:T(8,128)(2,1)S(1)}, bf16[64,3712]{1,0:T(8,128)(2,1)S(1)}, u32[]{:S(2)}, u32[]{:S(2)}) collective-permute-start(bf16[64,3712]{1,0:T(8,128)(2,1)S(1)} %collective-permute-done.3.refs_7_.refs_0_.refs_3_), channel_id=1, source_target_pairs={{0,2},{2,0},{4,6},{6,4},{8,10},{10,8},{12,14},{14,12},{16,18},{18,... | collective-permute-start | bytes 1425416 | tf_op jit(solution)/shard_map/ppermute | solution.py:205
  93.0 13.6 %collective-permute-start.24 = (bf16[64,3584]{1,0:T(8,128)(2,1)S(1)}, bf16[64,3584]{1,0:T(8,128)(2,1)S(1)}, u32[]{:S(2)}, u32[]{:S(2)}) collective-permute-start(bf16[64,3584]{1,0:T(8,128)(2,1)S(1)} %get-tuple-element.57), channel_id=1, source_target_pairs={{0,2},{2,0},{4,6},{6,4},{8,10},{10,8},{12,14},{14,12},{16,18},{18,... | collective-permute-start | bytes 1376264 | tf_op jit(solution)/shard_map/ppermute | solution.py:205
  93.5 13.1 %collective-permute-start.25 = (bf16[64,3584]{1,0:T(8,128)(2,1)S(1)}, bf16[64,3584]{1,0:T(8,128)(2,1)S(1)}, u32[]{:S(2)}, u32[]{:S(2)}) collective-permute-start(bf16[64,3584]{1,0:T(8,128)(2,1)S(1)} %add_convert_fusion.7.refs_7_), channel_id=1, source_target_pairs={{0,4},{2,6},{4,0},{6,2},{8,12},{10,14},{12,8},{14,10},{16,20},{18,... | collective-permute-start | bytes 1376264 | tf_op jit(solution)/shard_map/ppermute | solution.py:205
  95.0 8.8 %collective-permute-start.20 = (bf16[256,512]{1,0:T(8,128)(2,1)S(1)}, bf16[256,512]{1,0:T(8,128)(2,1)S(1)}, u32[]{:S(2)}, u32[]{:S(2)}) collective-permute-start(bf16[256,512]{1,0:T(8,128)(2,1)S(1)} %shard_map.132.refs_6_.refs_0_), channel_id=1, source_target_pairs={{0,1},{1,0},{2,3},{3,2},{4,5},{5,4},{6,7},{7,6},{8,9},{9,8},{10,11... | collective-permute-start | bytes 786440 | tf_op jit(solution)/shard_map/ppermute | solution.py:201
  96.3 32.8 %collective-permute-start.11 = (bf16[64,3584]{1,0:T(8,128)(2,1)S(1)}, bf16[64,3584]{1,0:T(8,128)(2,1)S(1)}, u32[]{:S(2)}, u32[]{:S(2)}) collective-permute-start(bf16[64,3584]{1,0:T(8,128)(2,1)S(1)} %get-tuple-element.45), channel_id=1, source_target_pairs={{0,2},{2,0},{4,6},{6,4},{8,10},{10,8},{12,14},{14,12},{16,18},{18,... | collective-permute-start | bytes 1376264 | tf_op jit(solution)/shard_map/ppermute | solution.py:205
  99.0 15.2 %collective-permute-start.27 = (bf16[2,256,512]{2,1,0:T(8,128)(2,1)S(1)}, bf16[2,256,512]{2,1,0:T(8,128)(2,1)S(1)}, u32[]{:S(2)}, u32[]{:S(2)}) collective-permute-start(bf16[2,256,512]{2,1,0:T(8,128)(2,1)S(1)} %shard_map.133.refs_7_), channel_id=1, source_target_pairs={{0,1},{1,0},{2,3},{3,2},{4,5},{5,4},{6,7},{7,6},{8,9},{9,8},{10,11... | collective-permute-start | bytes 1572872 | tf_op jit(solution)/shard_map/ppermute | solution.py:201
  106.6 10.5 %collective-permute-start.29 = (bf16[64,3584]{1,0:T(8,128)(2,1)S(1)}, bf16[64,3584]{1,0:T(8,128)(2,1)S(1)}, u32[]{:S(2)}, u32[]{:S(2)}) collective-permute-start(bf16[64,3584]{1,0:T(8,128)(2,1)S(1)} %get-tuple-element.55.refs_7_), channel_id=1, source_target_pairs={{0,2},{2,0},{4,6},{6,4},{8,10},{10,8},{12,14},{14,12},{16,18},{18,... | collective-permute-start | bytes 1376264 | tf_op jit(solution)/shard_map/ppermute | solution.py:205
  106.8 23.7 %collective-permute-start.30 = (bf16[64,3584]{1,0:T(8,128)(2,1)S(1)}, bf16[64,3584]{1,0:T(8,128)(2,1)S(1)}, u32[]{:S(2)}, u32[]{:S(2)}) collective-permute-start(bf16[64,3584]{1,0:T(8,128)(2,1)S(1)} %add_convert_fusion.6.refs_8_), channel_id=1, source_target_pairs={{0,16},{2,18},{4,20},{6,22},{8,24},{10,26},{12,28},{14,30},{16,0},... | collective-permute-start | bytes 1376264 | tf_op jit(solution)/shard_map/ppermute | solution.py:205
  108.3 20.9 %collective-permute-start.26 = (bf16[64,3584]{1,0:T(8,128)(2,1)S(1)}, bf16[64,3584]{1,0:T(8,128)(2,1)S(1)}, u32[]{:S(2)}, u32[]{:S(2)}) collective-permute-start(bf16[64,3584]{1,0:T(8,128)(2,1)S(1)} %add_convert_fusion.5.refs_9_), channel_id=1, source_target_pairs={{0,4},{2,6},{4,0},{6,2},{8,12},{10,14},{12,8},{14,10},{16,20},{18,... | collective-permute-start | bytes 1376264 | tf_op jit(solution)/shard_map/ppermute | solution.py:205
  114.3 18.4 %collective-permute-start.31 = (bf16[64,3584]{1,0:T(8,128)(2,1)S(1)}, bf16[64,3584]{1,0:T(8,128)(2,1)S(1)}, u32[]{:S(2)}, u32[]{:S(2)}) collective-permute-start(bf16[64,3584]{1,0:T(8,128)(2,1)S(1)} %get-tuple-element.67), channel_id=1, source_target_pairs={{0,2},{2,0},{4,6},{6,4},{8,10},{10,8},{12,14},{14,12},{16,18},{18,... | collective-permute-start | bytes 1376264 | tf_op jit(solution)/shard_map/ppermute | solution.py:205
  117.1 8.8 %collective-permute-start.28 = (bf16[256,512]{1,0:T(8,128)(2,1)S(1)}, bf16[256,512]{1,0:T(8,128)(2,1)S(1)}, u32[]{:S(2)}, u32[]{:S(2)}) collective-permute-start(bf16[256,512]{1,0:T(8,128)(2,1)S(1)} %shard_map.135.refs_0_.refs_7_), channel_id=1, source_target_pairs={{0,1},{1,0},{2,3},{3,2},{4,5},{5,4},{6,7},{7,6},{8,9},{9,8},{10,11... | collective-permute-start | bytes 786440 | tf_op jit(solution)/shard_map/ppermute | solution.py:201
  125.9 13.4 %collective-permute-start.32 = (bf16[64,3584]{1,0:T(8,128)(2,1)S(1)}, bf16[64,3584]{1,0:T(8,128)(2,1)S(1)}, u32[]{:S(2)}, u32[]{:S(2)}) collective-permute-start(bf16[64,3584]{1,0:T(8,128)(2,1)S(1)} %add_convert_fusion.4.refs_8_), channel_id=1, source_target_pairs={{0,4},{2,6},{4,0},{6,2},{8,12},{10,14},{12,8},{14,10},{16,20},{18,... | collective-permute-start | bytes 1376264 | tf_op jit(solution)/shard_map/ppermute | solution.py:205
  129.2 14.8 %collective-permute-start.35 = (bf16[64,3584]{1,0:T(8,128)(2,1)S(1)}, bf16[64,3584]{1,0:T(8,128)(2,1)S(1)}, u32[]{:S(2)}, u32[]{:S(2)}) collective-permute-start(bf16[64,3584]{1,0:T(8,128)(2,1)S(1)} %get-tuple-element.73), channel_id=1, source_target_pairs={{0,2},{2,0},{4,6},{6,4},{8,10},{10,8},{12,14},{14,12},{16,18},{18,... | collective-permute-start | bytes 1376264 | tf_op jit(solution)/shard_map/ppermute | solution.py:205
  131.1 16.7 %collective-permute-start.36 = (bf16[64,3584]{1,0:T(8,128)(2,1)S(1)}, bf16[64,3584]{1,0:T(8,128)(2,1)S(1)}, u32[]{:S(2)}, u32[]{:S(2)}) collective-permute-start(bf16[64,3584]{1,0:T(8,128)(2,1)S(1)} %add_convert_fusion.3), channel_id=1, source_target_pairs={{0,4},{2,6},{4,0},{6,2},{8,12},{10,14},{12,8},{14,10},{16,20},{18,... | collective-permute-start | bytes 1376264 | tf_op jit(solution)/shard_map/ppermute | solution.py:205
  139.5 14.9 %collective-permute-start.34 = (bf16[64,3584]{1,0:T(8,128)(2,1)S(1)}, bf16[64,3584]{1,0:T(8,128)(2,1)S(1)}, u32[]{:S(2)}, u32[]{:S(2)}) collective-permute-start(bf16[64,3584]{1,0:T(8,128)(2,1)S(1)} %add_convert_fusion.2), channel_id=1, source_target_pairs={{0,24},{2,26},{4,28},{6,30},{8,16},{10,18},{12,20},{14,22},{16,8},... | collective-permute-start | bytes 1376264 | tf_op jit(solution)/shard_map/ppermute | solution.py:205
  148.0 14.2 %collective-permute-start.37 = (bf16[64,3584]{1,0:T(8,128)(2,1)S(1)}, bf16[64,3584]{1,0:T(8,128)(2,1)S(1)}, u32[]{:S(2)}, u32[]{:S(2)}) collective-permute-start(bf16[64,3584]{1,0:T(8,128)(2,1)S(1)} %add_convert_fusion.1), channel_id=1, source_target_pairs={{0,8},{2,10},{4,12},{6,14},{8,0},{10,2},{12,4},{14,6},{16,24},{18,... | collective-permute-start | bytes 1376264 | tf_op jit(solution)/shard_map/ppermute | solution.py:205
  (6 other events, 23.2 us)
